TPU v7x, 32 devices: a whole 2x2x4 slice. The times are simulated.
32 devices in a mesh: groups: 2 (over y), pre: 4 (over z), dec: 4 (over x, core).
Axes of the slice: x: 2, y: 2, z: 4, core: 2. Of those that a mesh axis runs over, the one named last changes fastest.
Arguments:
- page_pool: bfloat16 [256, 128, 8, 2, 128], P(('groups', 'pre'), None, 'dec'), parts along dimension 0, may hold values from -4 to 4
- page_scales: bfloat16 [256, 8, 2], P(('groups', 'pre'), 'dec'), parts along dimension 0, may hold values from 0.5 to 2
- queries: bfloat16 [2, 256, 64, 128], P(None, ('groups', 'pre'), 'dec'), parts along dimension 1, may hold values from -48 to 48
- new_entries: bfloat16 [2, 256, 8, 2, 128], P(None, ('groups', 'pre'), 'dec'), parts along dimension 1, may hold values from -13 to 13
- token_cache: bfloat16 [256, 4, 8, 2, 128], P(('groups', 'pre'), None, 'dec'), parts along dimension 0, may hold values from -4 to 4
- cache_fill: int32 [256], P(('groups', 'pre')), parts along dimension 0, may hold values from 0 to 4
- page_counts: int32 [8, 2], P(('groups', 'pre')), parts along dimension 0, may hold values from 1 to 30, as said below
- page_table: int32 [8, 2, 30], P(('groups', 'pre')), parts along dimension 0, may hold values from -1 to 127, as said below
Outputs:
- attended: bfloat16 [2, 256, 64, 128], P(None, ('groups', 'pre'), 'dec'), parts along dimension 1
There are 2 independent parts, one for each index of `groups`. A program takes and returns all parts, laid end to end along the dimension named above; each array names one. Nothing has to cross between parts.
Inputs may be any that keep to these rules, and one draw needn't show every extreme that they name: `page_counts`: the 2 prompts of each decode group hold 32 pages together. page_table[g, q, j] for j < page_counts[g, q] is the pool row, owner index along pre times 32 plus a slot, of that page; -1 past the length. Every pool row holds exactly one page. Decode group g takes exactly 8 pages from each owner g - k (cyclic, k < 4) and none from other owners.
All inputs are finite; a program needn't handle non-finite values.
Results may differ from a plain program's by a relative error of at most 0.0021.
Values may be sent and summed in bfloat16 or wider, within the bound.
A program may use at most 128 MiB of HBM per device.

v0:
```python
import math

import jax
import jax.numpy as jnp
from jax import lax
from jax.sharding import PartitionSpec as P


def local_scores(grouped, cache_keys, fresh_keys, cache_fill, factor):
    cache_len = cache_keys.shape[2]
    step_count = fresh_keys.shape[1]
    cache_scores = (
        jnp.einsum("pctsgd,psicd->pctsgi", grouped, cache_keys, preferred_element_type=jnp.float32)
        * factor
    )
    present = (
        jnp.arange(cache_len, dtype=jnp.int32)[None, None, None, None, None, :]
        < cache_fill[:, None, None, :, None, None]
    )
    cache_scores = jnp.where(present, cache_scores, -jnp.inf)
    fresh_scores = (
        jnp.einsum("pctsgd,puscd->pctsgu", grouped, fresh_keys, preferred_element_type=jnp.float32)
        * factor
    )
    earlier = (
        jnp.arange(step_count, dtype=jnp.int32)[:, None]
        >= jnp.arange(step_count, dtype=jnp.int32)[None, :]
    )
    fresh_scores = jnp.where(earlier[None, None, :, None, None, :], fresh_scores, -jnp.inf)
    return (cache_scores, fresh_scores)


def local_terms(row_peak, cache_scores, fresh_scores, cache_values, fresh_values):
    cache_exp = jnp.exp(cache_scores - row_peak[..., None])
    fresh_exp = jnp.exp(fresh_scores - row_peak[..., None])
    denominator = jnp.sum(cache_exp, axis=-1) + jnp.sum(fresh_exp, axis=-1)
    mixed = jnp.einsum(
        "pctsgi,psicd->pctsgd",
        cache_exp.astype(jnp.bfloat16),
        cache_values,
        preferred_element_type=jnp.float32,
    )
    mixed = mixed + jnp.einsum(
        "pctsgu,puscd->pctsgd",
        fresh_exp.astype(jnp.bfloat16),
        fresh_values,
        preferred_element_type=jnp.float32,
    )
    return (denominator, mixed)


def request_table(group_table, lengths, pool_rows, pre_count, capacity):
    prompts, page_most = group_table.shape
    is_live = lax.broadcasted_iota(jnp.int32, (prompts, page_most), 1) < lengths[:, None]
    flat_ids = jnp.where(is_live, group_table, 0).reshape(-1)
    flat_live = is_live.reshape(-1)
    owners = jnp.where(flat_live, flat_ids // pool_rows, -1)
    pool_slots = flat_ids % pool_rows
    owner_hit = (owners[:, None] == lax.broadcasted_iota(jnp.int32, (1, pre_count), 1)).astype(
        jnp.int32
    )
    before = jnp.cumsum(owner_hit, axis=0) - owner_hit
    owner_rank = jnp.sum(before * owner_hit, axis=1)
    rank_hit = (owner_rank[:, None] == lax.broadcasted_iota(jnp.int32, (1, capacity), 1)).astype(
        jnp.int32
    )
    wanted = owner_hit[:, :, None] * rank_hit[:, None, :]
    requests = jnp.sum(wanted * (pool_slots + 1)[:, None, None], axis=0) - 1
    return (requests, owners, owner_rank, flat_live)


def pick_pages(page_pool, page_scales, wanted):
    flat_rows = jnp.maximum(wanted, 0).reshape(-1)
    page_block = jnp.take(page_pool, flat_rows, axis=0).reshape(wanted.shape + page_pool.shape[1:])
    scale_block = jnp.take(page_scales, flat_rows, axis=0).reshape(
        wanted.shape + page_scales.shape[1:]
    )
    return (page_block, scale_block)


def shards(
    page_pool, page_scales, queries, new_entries, token_cache, cache_fill, page_counts, page_table
):
    pre_count = lax.axis_size("pre")
    pool_rows = page_pool.shape[0]
    capacity = max(1, pool_rows // pre_count)
    kv_count = page_pool.shape[2]
    step_count, row_count, head_count, head_width = queries.shape
    prompts = page_counts.shape[1]
    page_most = page_table.shape[2]
    samples = row_count // prompts
    cache_len = token_cache.shape[1]
    head_ratio = head_count // kv_count
    factor = 1.0 / math.sqrt(head_width)
    requests, owners, owner_rank, flat_live = request_table(
        page_table[0], page_counts[0], pool_rows, pre_count, capacity
    )
    incoming = lax.all_to_all(requests, "pre", split_axis=0, concat_axis=0, tiled=True)
    page_block, scale_block = pick_pages(page_pool, page_scales, incoming)
    arrived, arrived_scales = (
        lax.all_to_all(page_block, "pre", split_axis=0, concat_axis=0, tiled=True),
        lax.all_to_all(scale_block, "pre", split_axis=0, concat_axis=0, tiled=True),
    )
    places = owners * capacity + owner_rank
    places = jnp.where(flat_live, places, 0)
    arrived = arrived.reshape((-1,) + page_pool.shape[1:])
    arrived_scales = arrived_scales.reshape((-1,) + page_scales.shape[1:])
    grouped = queries.reshape(
        step_count, prompts, samples, kv_count, head_ratio, head_width
    ).transpose(1, 3, 0, 2, 4, 5)
    cache_all = token_cache.reshape(prompts, samples, cache_len, kv_count, 2, head_width)
    fresh_all = new_entries.reshape(
        step_count, prompts, samples, kv_count, 2, head_width
    ).transpose(1, 0, 2, 3, 4, 5)
    filled = cache_fill.reshape(prompts, samples)
    cache_values = cache_all[..., 1, :]
    fresh_values = fresh_all[..., 1, :]
    cache_scores, fresh_scores = local_scores(
        grouped, cache_all[..., 0, :], fresh_all[..., 0, :], filled, factor
    )
    page_spots = places.reshape(prompts, page_most)
    live_pages = flat_live.reshape(prompts, page_most)

    def prompt_block(inputs):
        page_spot, live_row, prompt_query, cache_part, fresh_part, cache_vals, fresh_vals = inputs
        chosen = jnp.take(arrived, page_spot, axis=0)
        chosen_scales = jnp.take(arrived_scales, page_spot, axis=0).astype(jnp.float32)
        key_scale = chosen_scales[:, :, 0].T[:, None, None, None, :, None]
        prefix_scores = (
            jnp.einsum(
                "ctsgd,jicd->ctsgji",
                prompt_query,
                chosen[:, :, :, 0, :],
                preferred_element_type=jnp.float32,
            )
            * factor
            * key_scale
        )
        prefix_scores = jnp.where(live_row[:, None], prefix_scores, -jnp.inf)
        row_peak = jnp.maximum(
            jnp.max(prefix_scores, axis=(-2, -1)),
            jnp.maximum(jnp.max(cache_part, axis=-1), jnp.max(fresh_part, axis=-1)),
        )
        denominator, mixed = local_terms(
            row_peak[None], cache_part[None], fresh_part[None], cache_vals[None], fresh_vals[None]
        )
        prefix_exp = jnp.exp(prefix_scores - row_peak[..., None, None])
        denominator = denominator[0] + jnp.sum(prefix_exp, axis=(-2, -1))
        value_scale = chosen_scales[:, :, 1].T[:, None, None, None, :, None]
        per_page = jnp.einsum(
            "ctsgji,jicd->ctsgjd",
            prefix_exp.astype(jnp.bfloat16),
            chosen[:, :, :, 1, :],
            preferred_element_type=jnp.float32,
        )
        mixed = mixed[0] + jnp.sum(per_page * value_scale, axis=-2)
        return (mixed / denominator[..., None]).astype(jnp.bfloat16)

    result = lax.map(
        prompt_block,
        (page_spots, live_pages, grouped, cache_scores, fresh_scores, cache_values, fresh_values),
    )
    return result.transpose(2, 0, 3, 1, 4, 5).reshape(step_count, row_count, head_count, head_width)


def solution(mesh):
    in_specs = (
        P(("groups", "pre"), None, "dec", None, None),
        P(("groups", "pre"), "dec", None),
        P(None, ("groups", "pre"), "dec", None),
        P(None, ("groups", "pre"), "dec", None, None),
        P(("groups", "pre"), None, "dec", None, None),
        P(("groups", "pre")),
        P(("groups", "pre"), None),
        P(("groups", "pre"), None, None),
    )
    out_specs = P(None, ("groups", "pre"), "dec", None)
    return jax.shard_map(shards, mesh=mesh, in_specs=in_specs, out_specs=out_specs, check_vma=False)
```

profile of v0, /device:TPU:0, one launch (start us, length us, event | category | flops | bytes accessed | tf_op | source)
XLA Modules:
  0.0 182.3 jit_solution(9950762150358822311)
XLA Ops:
  0.8 0.8 squeeze.52
  2.8 6.3 %all-to-all-start = ((s32[4,1,8]{2,1,0:T(1,128)}), s32[4,1,8]{2,1,0:T(1,128)S(1)}, u32[]{:S(2)}, u32[]{:S(2)}) async-start(s32[4,1,8]{2,1,0:T(1,128)} %bitcast.41), calls=%async_computation | async-start | bytes 4096 | tf_op jit(solution)/shard_map/all_to_all | solution.py:98
  9.1 0.8 copy.150
  9.9 4.7 %all-to-all-done = s32[4,1,8]{2,1,0:T(1,128)S(1)} async-done(((s32[4,1,8]{2,1,0:T(1,128)}), s32[4,1,8]{2,1,0:T(1,128)S(1)}, u32[]{:S(2)}, u32[]{:S(2)}) %all-to-all-start) | async-done | bytes 160 | tf_op jit(solution)/shard_map/all_to_all | solution.py:98
  14.7 12.3 %gather_fusion.2 = bf16[32,128,2,2,128]{4,3,2,1,0:T(2,128)(2,1)} fusion(bf16[32,128,2,2,128]{4,3,2,1,0:T(2,128)(2,1)} %param.10, s32[1024]{0:T(1024)S(1)} %pad_clamp_fusion.1), kind=kCustom, calls=%fused_computation.2 | custom fusion | bytes 8388736 | tf_op jit(solution)/shard_map/jit(_take)/gather | solution.py:74
  28.4 3.2 %all-to-all-start.2 = ((bf16[4,8,2,2]{1,3,2,0:T(2,128)(2,1)}), bf16[4,8,2,2]{1,3,2,0:T(2,128)(2,1)S(1)}, u32[]{:S(2)}, u32[]{:S(2)}) async-start(bf16[4,8,2,2]{1,3,2,0:T(2,128)(2,1)} %copy.152), calls=%async_computation.2 | async-start | bytes 8192 | tf_op jit(solution)/shard_map/all_to_all | solution.py:102
  31.7 4.7 %copy_select_fusion.1 = bf16[4,8,128,2,2,128]{5,2,4,3,1,0:T(8,128)(2,1)} fusion(bf16[4,8,128,2,2,128]{5,4,3,2,1,0:T(2,128)(2,1)} %bitcast.149, pred[4,8]{1,0:T(4,128)(4,1)S(1)} %bitcast.161), kind=kLoop, calls=%fused_computation.57 | loop fusion | flops 2097152 | bytes 8388640 | tf_op jit(solution)/shard_map/jit(_take)/select_n | solution.py:74
  36.4 0.8 all-to-all-done.2
  37.2 4.9 %all-to-all-start.1 = ((bf16[4,8,128,2,2,128]{5,2,4,3,1,0:T(8,128)(2,1)}), bf16[4,8,128,2,2,128]{5,2,4,3,1,0:T(8,128)(2,1)}, u32[]{:S(2)}, u32[]{:S(2)}) async-start(bf16[4,8,128,2,2,128]{5,2,4,3,1,0:T(8,128)(2,1)} %copy_select_fusion.1), calls=%async_computation.1 | async-start | bytes 8388608 | tf_op jit(solution)/shard_map/all_to_all | solution.py:101
  42.7 1.2 fusion.33
  43.9 1.3 fusion.31
  45.3 88.2 %all-to-all-done.1 = bf16[4,8,128,2,2,128]{5,2,4,3,1,0:T(8,128)(2,1)} async-done(((bf16[4,8,128,2,2,128]{5,2,4,3,1,0:T(8,128)(2,1)}), bf16[4,8,128,2,2,128]{5,2,4,3,1,0:T(8,128)(2,1)}, u32[]{:S(2)}, u32[]{:S(2)}) %all-to-all-start.1) | async-done | bytes 4194336 | tf_op jit(solution)/shard_map/all_to_all | solution.py:101
  133.5 48.0 %while.10 = (s32[]{:T(128)}, bf16[2,2,2,16,8,128]{5,4,2,3,1,0:T(8,128)(2,1)S(1)}, bf16[2,16,4,2,128]{4,1,0,3,2:T(8,128)(2,1)S(1)}, f32[2,2,2,16,8,4]{4,5,2,3,1,0...) while((s32[]{:T(128)}, ...), condition=%wide.region_11.12_spmd, body=%wide.region_3.11_spmd.sunk | while | flops 1029258816 | bytes 60793964 | solution.py:159
  134.3 5.1 %gather_fusion.1 = bf16[30,128,2,2,128]{4,1,3,2,0:T(8,128)(2,1)} fusion(bf16[32,128,2,2,128]{4,1,3,2,0:T(8,128)(2,1)} %get-tuple-element.271, s32[1024]{0:T(1024)S(1)} %pad_clamp_fusion.3), kind=kCustom, calls=%fused_computation.clone.1 | custom fusion | bytes 7864440 | tf_op jit(solution)/shard_map/while/body/eval_jaxpr/jit(_take)/gather | solution.py:126
  139.4 2.5 %copy_select_fusion.3 = bf16[30,128,2,2,128]{4,1,0,2,3:T(8,128)(2,1)S(1)} fusion(bf16[30,128,2,2,128]{4,1,3,2,0:T(8,128)(2,1)} %gather_fusion.1, pred[30]{0:T(512)(128)(4,1)S(1)} %compare_and_fusion.2), kind=kLoop, calls=%fused_computation.12.clone.1 | loop fusion | flops 1966080 | bytes 7864350 | tf_op jit(solution)/shard_map/while/body/eval_jaxpr/jit(_take)/select_n | solution.py:126
  142.0 4.3 %fusion.61 = (f32[2,2,16,8]{3,2,1,0:T(8,128)S(1)}, f32[2,2,16,8,30,128]{5,3,4,2,1,0:T(8,128)}) fusion(f32[2,30]{1,0:T(2,128)S(1)} %get-tuple-element.234, pred[30]{0:T(512)(128)(4,1)S(1)} %fusion.60, bf16[30,128,2,2,128]{4,1,0,2,3:T(8,128)(2,1)S(1)} %copy_select_fusion.3, bf16[2,2,2,16,8,128]{5,4,1,3,0,2:T(8,128)(2,1)S(1)} %get-tuple-element.269, ...), kind=kOutput, calls=%fused_computation.7.clone.1 | convolution fusion | flops 509214208 | bytes 9965060 | tf_op jit(solution)/shard_map/while/body/eval_jaxpr/ctsgd,jicd->ctsgji/dot_general | solution.py:130
  146.9 5.7 %fusion.63 = (f32[2,2,16,8]{3,2,1,0:T(8,128)S(1)}, bf16[2,2,16,8,30,128]{5,3,4,2,1,0:T(8,128)(2,1)}) fusion(f32[2,2,16,8,30,128]{5,3,4,2,1,0:T(8,128)} %get-tuple-element.237, f32[2,2,16,8]{3,2,1,0:T(8,128)S(1)} %copy.224, f32[2,30]{1,0:T(2,128)S(1)} %get-tuple-element.234, pred[30]{0:T(512)(128)(4,1)S(1)} %fusion.60), kind=kLoop, calls=%fused_computation.8.clone.1 | loop fusion | flops 9829888 | bytes 11800846 | tf_op jit(solution)/shard_map/while/body/eval_jaxpr/reduce_sum | solution.py:148
  153.0 3.9 %multiply_reduce_fusion.3 = f32[2,128,2,16,8]{1,3,4,2,0:T(8,128)S(1)} fusion(f32[2,30]{1,0:T(2,128)S(1)} %get-tuple-element.236, bf16[2,2,16,8,30,128]{5,3,4,2,1,0:T(8,128)(2,1)} %get-tuple-element.238, bf16[30,128,2,2,128]{4,1,0,2,3:T(8,128)(2,1)} %copy-done), kind=kOutput, calls=%fused_computation.4.clone.1 | convolution fusion | flops 507183104 | bytes 6160624 | tf_op jit(solution)/shard_map/while/body/eval_jaxpr/ctsgji,jicd->ctsgjd/dot_general | solution.py:150
  158.3 5.1 %gather_fusion.1 = bf16[30,128,2,2,128]{4,1,3,2,0:T(8,128)(2,1)} fusion(bf16[32,128,2,2,128]{4,1,3,2,0:T(8,128)(2,1)} %get-tuple-element.271, s32[1024]{0:T(1024)S(1)} %pad_clamp_fusion.3), kind=kCustom, calls=%fused_computation.clone.1 | custom fusion | bytes 7864440 | tf_op jit(solution)/shard_map/while/body/eval_jaxpr/jit(_take)/gather | solution.py:126
  163.5 2.5 %copy_select_fusion.3 = bf16[30,128,2,2,128]{4,1,0,2,3:T(8,128)(2,1)S(1)} fusion(bf16[30,128,2,2,128]{4,1,3,2,0:T(8,128)(2,1)} %gather_fusion.1, pred[30]{0:T(512)(128)(4,1)S(1)} %compare_and_fusion.2), kind=kLoop, calls=%fused_computation.12.clone.1 | loop fusion | flops 1966080 | bytes 7864350 | tf_op jit(solution)/shard_map/while/body/eval_jaxpr/jit(_take)/select_n | solution.py:126
  166.1 4.3 %fusion.61 = (f32[2,2,16,8]{3,2,1,0:T(8,128)S(1)}, f32[2,2,16,8,30,128]{5,3,4,2,1,0:T(8,128)}) fusion(f32[2,30]{1,0:T(2,128)S(1)} %get-tuple-element.234, pred[30]{0:T(512)(128)(4,1)S(1)} %fusion.60, bf16[30,128,2,2,128]{4,1,0,2,3:T(8,128)(2,1)S(1)} %copy_select_fusion.3, bf16[2,2,2,16,8,128]{5,4,1,3,0,2:T(8,128)(2,1)S(1)} %get-tuple-element.269, ...), kind=kOutput, calls=%fused_computation.7.clone.1 | convolution fusion | flops 509214208 | bytes 9965060 | tf_op jit(solution)/shard_map/while/body/eval_jaxpr/ctsgd,jicd->ctsgji/dot_general | solution.py:130
  170.9 5.7 %fusion.63 = (f32[2,2,16,8]{3,2,1,0:T(8,128)S(1)}, bf16[2,2,16,8,30,128]{5,3,4,2,1,0:T(8,128)(2,1)}) fusion(f32[2,2,16,8,30,128]{5,3,4,2,1,0:T(8,128)} %get-tuple-element.237, f32[2,2,16,8]{3,2,1,0:T(8,128)S(1)} %copy.224, f32[2,30]{1,0:T(2,128)S(1)} %get-tuple-element.234, pred[30]{0:T(512)(128)(4,1)S(1)} %fusion.60), kind=kLoop, calls=%fused_computation.8.clone.1 | loop fusion | flops 9829888 | bytes 11800846 | tf_op jit(solution)/shard_map/while/body/eval_jaxpr/reduce_sum | solution.py:148
  177.0 3.9 %multiply_reduce_fusion.3 = f32[2,128,2,16,8]{1,3,4,2,0:T(8,128)S(1)} fusion(f32[2,30]{1,0:T(2,128)S(1)} %get-tuple-element.236, bf16[2,2,16,8,30,128]{5,3,4,2,1,0:T(8,128)(2,1)} %get-tuple-element.238, bf16[30,128,2,2,128]{4,1,0,2,3:T(8,128)(2,1)} %copy-done), kind=kOutput, calls=%fused_computation.4.clone.1 | convolution fusion | flops 507183104 | bytes 6160624 | tf_op jit(solution)/shard_map/while/body/eval_jaxpr/ctsgji,jicd->ctsgjd/dot_general | solution.py:150
  181.6 0.7 copy.160
  (91 shorter events, 8.7 us)
Async XLA Ops:
  2.8 11.8 %all-to-all-start = ((s32[4,1,8]{2,1,0:T(1,128)}), s32[4,1,8]{2,1,0:T(1,128)S(1)}, u32[]{:S(2)}, u32[]{:S(2)}) async-start(s32[4,1,8]{2,1,0:T(1,128)} %bitcast.41), calls=%async_computation | async-start | bytes 4096 | tf_op jit(solution)/shard_map/all_to_all | solution.py:98
  28.4 8.8 %all-to-all-start.2 = ((bf16[4,8,2,2]{1,3,2,0:T(2,128)(2,1)}), bf16[4,8,2,2]{1,3,2,0:T(2,128)(2,1)S(1)}, u32[]{:S(2)}, u32[]{:S(2)}) async-start(bf16[4,8,2,2]{1,3,2,0:T(2,128)(2,1)} %copy.152), calls=%async_computation.2 | async-start | bytes 8192 | tf_op jit(solution)/shard_map/all_to_all | solution.py:102
  36.4 5.9 %copy-start.2 = (bf16[32,4,2,2,128]{4,3,2,1,0:T(2,128)(2,1)S(1)}, bf16[32,4,2,2,128]{4,3,2,1,0:T(2,128)(2,1)}, u32[]{:S(2)}) copy-start(bf16[32,4,2,2,128]{4,3,2,1,0:T(2,128)(2,1)} %param.14) | copy-start | bytes 393220
  36.4 5.9 %copy-start.6 = (s32[32]{0:T(128)S(1)}, s32[32]{0:T(128)}, u32[]{:S(2)}) copy-start(s32[32]{0:T(128)} %param.15) | copy-start | bytes 388
  36.4 6.0 %copy-start.3 = (bf16[2,32,2,2,128]{4,3,2,1,0:T(2,128)(2,1)S(1)}, bf16[2,32,2,2,128]{4,3,2,1,0:T(2,128)(2,1)}, u32[]{:S(2)}) copy-start(bf16[2,32,2,2,128]{4,3,2,1,0:T(2,128)(2,1)} %param.13) | copy-start | bytes 196612
  36.4 6.1 %copy-start.4 = (s32[1,2,30]{2,1,0:T(2,128)S(1)}, s32[1,2,30]{2,1,0:T(2,128)}, u32[]{:S(2)}) copy-start(s32[1,2,30]{2,1,0:T(2,128)} %param.17) | copy-start | bytes 724
  36.4 6.1 %copy-start.5 = (s32[1,2]{1,0:T(1,128)S(1)}, s32[1,2]{1,0:T(1,128)}, u32[]{:S(2)}) copy-start(s32[1,2]{1,0:T(1,128)} %param.16) | copy-start | bytes 28
  36.4 6.3 %copy-start.1 = (bf16[2,32,16,128]{3,2,1,0:T(8,128)(2,1)S(1)}, bf16[2,32,16,128]{3,2,1,0:T(8,128)(2,1)}, u32[]{:S(2)}) copy-start(bf16[2,32,16,128]{3,2,1,0:T(8,128)(2,1)} %param.12) | copy-start | bytes 786436
  37.2 96.3 %all-to-all-start.1 = ((bf16[4,8,128,2,2,128]{5,2,4,3,1,0:T(8,128)(2,1)}), bf16[4,8,128,2,2,128]{5,2,4,3,1,0:T(8,128)(2,1)}, u32[]{:S(2)}, u32[]{:S(2)}) async-start(bf16[4,8,128,2,2,128]{5,2,4,3,1,0:T(8,128)(2,1)} %copy_select_fusion.1), calls=%async_computation.1 | async-start | bytes 8388608 | tf_op jit(solution)/shard_map/all_to_all | solution.py:101
  142.0 4.4 %copy-start = (bf16[30,128,2,2,128]{4,1,0,2,3:T(8,128)(2,1)}, bf16[30,128,2,2,128]{4,1,0,2,3:T(8,128)(2,1)S(1)}, u32[]{:S(2)}) copy-start(bf16[30,128,2,2,128]{4,1,0,2,3:T(8,128)(2,1)S(1)} %copy_select_fusion.3) | copy-start | bytes 11796484 | tf_op jit(solution)/shard_map/while
  166.0 4.4 %copy-start = (bf16[30,128,2,2,128]{4,1,0,2,3:T(8,128)(2,1)}, bf16[30,128,2,2,128]{4,1,0,2,3:T(8,128)(2,1)S(1)}, u32[]{:S(2)}) copy-start(bf16[30,128,2,2,128]{4,1,0,2,3:T(8,128)(2,1)S(1)} %copy_select_fusion.3) | copy-start | bytes 11796484 | tf_op jit(solution)/shard_map/while
where the time goes:
time: 183 us; the launch traced here: 182 us
  waiting for transfers between devices  93.7 us (51%)
  local copies, waits for them, and re-layouts  29.2 us (16%)
  other arithmetic  24.4 us (13%)
  matrix products  20.1 us (11%)
  starting transfers between devices  14.5 us (8%)
    all_to_all x1, waiting for transfers between devices, shards(): lax.all_to_all(page_block, 'pre', split_axis=0, concat_axis=0, tiled=True)  88.2 us
    gather x1, local copies, waits for them, and re-layouts, pick_pages(): jnp.take(page_pool, flat_rows, axis=0)  12.3 us
    reduce_sum x2, other arithmetic, prompt_block(): denominator = denominator[0] + jnp.sum(prefix_exp, axis=(-2, -1))  11.4 us
    gather x2, local copies, waits for them, and re-layouts, prompt_block(): chosen = jnp.take(arrived, page_spot, axis=0)  10.3 us
    dot_general x2, matrix products, prompt_block(): jnp.einsum('ctsgd,jicd->ctsgji', prompt_query, chosen[:, :, :, 0, :], pre...  8.66 us
    dot_general x2, matrix products, prompt_block(): jnp.einsum('ctsgji,jicd->ctsgjd', prefix_exp.astype(jnp.bfloat16), chosen...  7.82 us
    all_to_all x1, starting transfers between devices, shards(): lax.all_to_all(requests, 'pre', split_axis=0, concat_axis=0, tiled=True)  6.32 us
    select_n x4, other arithmetic, prompt_block(): chosen = jnp.take(arrived, page_spot, axis=0)  5.11 us
  transfers between devices with their start and end apart: 3, of which 3 were waited for; matrix products, arithmetic and copies ran while one was open for 5% of the time, Pallas kernels for 0%

commit v1 on v0

--- a/solution.py
+++ b/solution.py
@@ -1,8 +1,11 @@
+import functools
 import math
 
 import jax
 import jax.numpy as jnp
 from jax import lax
+from jax.experimental import pallas as pl
+from jax.experimental.pallas import tpu as pltpu
 from jax.sharding import PartitionSpec as P
 
 
@@ -78,7 +81,7 @@
     return (page_block, scale_block)
 
 
-def shards(
+def move_pages(
     page_pool, page_scales, queries, new_entries, token_cache, cache_fill, page_counts, page_table
 ):
     pre_count = lax.axis_size("pre")
@@ -163,6 +166,388 @@
     return result.transpose(2, 0, 3, 1, 4, 5).reshape(step_count, row_count, head_count, head_width)
 
 
+MESH = pl.DeviceIdType.MESH
+LOW = -1e30
+FULL = 32000.0
+
+
+def partner_of(me, k, count):
+    bit, result = 1, 0
+    while bit < count:
+        result = result + ((me // bit) % 2 + (k // bit) % 2) % 2 * bit
+        bit *= 2
+    return result
+
+
+def request_kernel(pool_rows, counts_ref, table_ref, out_ref, rank_ref):
+    for owner in range(out_ref.shape[0]):
+        rank_ref[owner] = 0
+    for prompt in range(table_ref.shape[1]):
+
+        def place(j, carry, prompt=prompt):
+            page = table_ref[0, prompt, j]
+            owner = page // pool_rows
+            rank = rank_ref[owner]
+            out_ref[owner, rank] = (page - owner * pool_rows) * 2 + prompt
+            rank_ref[owner] = rank + 1
+            return carry
+
+        lax.fori_loop(0, counts_ref[0, prompt], place, 0)
+
+
+def nt_dot(a, b):
+    return lax.dot_general(a, b, (((1,), (1,)), ((), ())), preferred_element_type=jnp.float32)
+
+
+def attend_kernel(
+    dims,
+    request_ref,
+    scale_ref,
+    fill_ref,
+    queries_ref,
+    cache_ref,
+    fresh_ref,
+    pool_ref,
+    out_ref,
+    raw,
+    keys,
+    values,
+    asked,
+    asked_smem,
+    query_slots,
+    query_now,
+    scores,
+    sums,
+    part_out,
+    part_in,
+    stat_out,
+    stat_in,
+    local_sum,
+    local_stat,
+    turned,
+    pool_sem,
+    smem_sem,
+    ask_send,
+    ask_recv,
+    query_send,
+    query_recv,
+    part_send,
+    part_recv,
+    stat_send,
+    stat_recv,
+):
+    count, capacity, factor = dims
+    pages = raw.shape[0]
+    me = lax.axis_index("pre")
+    partners = [partner_of(me, k, count) for k in range(count)]
+
+    barrier = pltpu.get_barrier_semaphore()
+    for k in range(1, count):
+        pl.semaphore_signal(barrier, inc=1, device_id={"pre": partners[k]}, device_id_type=MESH)
+    pool_copy = pltpu.make_async_copy(pool_ref, raw, pool_sem)
+    pool_copy.start()
+    own_ask = pltpu.make_async_copy(request_ref.at[me], asked_smem.at[0], smem_sem.at[0])
+    own_ask.start()
+
+    for prompt in range(2):
+        for step in range(2):
+            block = queries_ref[step, prompt * 16 : prompt * 16 + 16].astype(jnp.float32)
+            for c in range(2):
+                rows = block[:, c * 8 : c * 8 + 8, :].reshape(128, 128)
+                query_slots[0, c, prompt, step * 128 : step * 128 + 128, :] = rows.astype(
+                    jnp.bfloat16
+                )
+    pl.semaphore_wait(barrier, count - 1)
+
+    def ask_copy(k, target):
+        return pltpu.make_async_remote_copy(
+            src_ref=request_ref.at[target],
+            dst_ref=asked.at[k],
+            send_sem=ask_send.at[k],
+            recv_sem=ask_recv.at[k],
+            device_id={"pre": target},
+            device_id_type=MESH,
+        )
+
+    def query_copy(k, c, target):
+        return pltpu.make_async_remote_copy(
+            src_ref=query_slots.at[0, c],
+            dst_ref=query_slots.at[k, c],
+            send_sem=query_send.at[k, c],
+            recv_sem=query_recv.at[k, c],
+            device_id={"pre": target},
+            device_id_type=MESH,
+        )
+
+    def part_copy(k, c, target):
+        return pltpu.make_async_remote_copy(
+            src_ref=part_out.at[k, c],
+            dst_ref=part_in.at[k, c],
+            send_sem=part_send.at[k, c],
+            recv_sem=part_recv.at[k, c],
+            device_id={"pre": target},
+            device_id_type=MESH,
+        )
+
+    def stat_copy(k, c, target):
+        return pltpu.make_async_remote_copy(
+            src_ref=stat_out.at[k, c],
+            dst_ref=stat_in.at[k, c],
+            send_sem=stat_send.at[k, c],
+            recv_sem=stat_recv.at[k, c],
+            device_id={"pre": target},
+            device_id_type=MESH,
+        )
+
+    for k in range(1, count):
+        ask_copy(k, partners[k]).start()
+    for c in range(2):
+        for k in range(1, count):
+            query_copy(k, c, partners[k]).start()
+
+    to_row = lax.broadcasted_iota(jnp.int32, (256, 256), 0)
+    from_row = lax.broadcasted_iota(jnp.int32, (256, 256), 1)
+    order = jnp.where(from_row == (to_row % 64) * 4 + to_row // 64, 1.0, 0.0).astype(jnp.bfloat16)
+
+    def sort_rows(block):
+        return jnp.dot(order, block, preferred_element_type=jnp.float32)
+
+    fresh_block = jnp.concatenate(
+        [
+            fresh_ref[step * 128 + prompt * 64 : step * 128 + prompt * 64 + 64, :]
+            for prompt in range(2)
+            for step in range(2)
+        ],
+        axis=0,
+    )
+    fresh_rows = sort_rows(fresh_block)
+    key_at = lax.broadcasted_iota(jnp.int32, (128, 256), 0)
+    query_at = lax.broadcasted_iota(jnp.int32, (128, 256), 1)
+    query_sample = (query_at // 8) % 16
+    is_cache = key_at < 64
+    is_fresh = (key_at >= 64) & (key_at < 96)
+    fresh_ok = is_fresh & (key_at % 16 == query_sample) & ((key_at - 64) // 16 <= query_at // 128)
+    cache_same = is_cache & (key_at // 4 == query_sample)
+    for prompt in range(2):
+        cache_rows = sort_rows(cache_ref[prompt * 256 : prompt * 256 + 256, :])
+        filled = jnp.zeros((128, 256), jnp.int32)
+        for sample in range(16):
+            filled = jnp.where(query_sample == sample, fill_ref[prompt * 16 + sample], filled)
+        present = (cache_same & (key_at % 4 < filled)) | fresh_ok
+        for c in range(2):
+
+            def pick(kind):
+                at = (c * 2 + kind) * 64
+                return jnp.concatenate(
+                    [
+                        cache_rows[at : at + 64],
+                        fresh_rows[at + prompt * 32 : at + prompt * 32 + 32],
+                        jnp.zeros((32, 128), jnp.float32),
+                    ],
+                    axis=0,
+                )
+
+            part = nt_dot(pick(0).astype(jnp.bfloat16), query_slots[0, c, prompt]) * factor
+            part = jnp.where(present, part, LOW)
+            peak = jnp.max(part, axis=0, keepdims=True)
+            grown = jnp.exp(part - peak)
+            local_stat[c, prompt, 0:1, :] = peak
+            local_stat[c, prompt, 1:2, :] = jnp.sum(grown, axis=0, keepdims=True)
+            local_sum[c, prompt] = jnp.dot(
+                pick(1).T.astype(jnp.bfloat16),
+                grown.astype(jnp.bfloat16),
+                preferred_element_type=jnp.float32,
+            )
+
+    pool_copy.wait()
+
+    def sort_page(page, carry):
+        halves = [sort_rows(raw[page, h * 256 : h * 256 + 256, :]) for h in range(2)]
+        for c in range(2):
+            at = c * 128
+            keys[page, c] = jnp.concatenate([x[at : at + 64] for x in halves], axis=0).astype(
+                jnp.bfloat16
+            )
+            values[page, c] = jnp.concatenate(
+                [x[at + 64 : at + 128] for x in halves], axis=0
+            ).T.astype(jnp.bfloat16)
+        return carry
+
+    lax.fori_loop(0, pages, sort_page, 0)
+    own_ask.wait()
+
+    def serve(index, carry):
+        c, k = index // count, index % count
+        target = partner_of(me, k, count)
+
+        @pl.when((c == 0) & (k > 0))
+        def _():
+            ask_copy(k, target).wait_recv()
+            to_smem = pltpu.make_async_copy(asked.at[k], asked_smem.at[k], smem_sem.at[k])
+            to_smem.start()
+            to_smem.wait()
+
+        @pl.when(k > 0)
+        def _():
+            query_copy(k, c, target).wait_recv()
+
+        query_now[...] = query_slots[k, c]
+        codes = [asked_smem[k, 0, j] for j in range(capacity)]
+        slots = [code // 2 for code in codes]
+        prompts = [code % 2 for code in codes]
+        peaks = [jnp.full((1, 256), LOW, jnp.float32) for _ in range(2)]
+        for j in range(capacity):
+            key_scale = scale_ref[c * 2 * pages + slots[j]] * factor
+            part = nt_dot(keys[slots[j], c], query_now[prompts[j]]) * key_scale
+            scores[j] = part
+            peak = jnp.max(part, axis=0, keepdims=True)
+            for p in range(2):
+                peaks[p] = jnp.maximum(peaks[p], jnp.where(prompts[j] == p, peak, LOW))
+        totals = [jnp.zeros((1, 256), jnp.float32) for _ in range(2)]
+        sums[...] = jnp.zeros_like(sums)
+        for j in range(capacity):
+            peak = jnp.where(prompts[j] == 0, peaks[0], peaks[1])
+            grown = jnp.exp(scores[j] - peak)
+            total = jnp.sum(grown, axis=0, keepdims=True)
+            mixed = jnp.dot(
+                values[slots[j], c],
+                grown.astype(jnp.bfloat16),
+                preferred_element_type=jnp.float32,
+            )
+            value_scale = scale_ref[(c * 2 + 1) * pages + slots[j]]
+            for p in range(2):
+                totals[p] = totals[p] + jnp.where(prompts[j] == p, total, 0.0)
+                sums[p] = sums[p] + mixed * jnp.where(prompts[j] == p, value_scale, 0.0)
+        for p in range(2):
+            mixed = sums[p]
+            largest = jnp.max(jnp.abs(mixed), axis=0, keepdims=True)
+            coded = jnp.round(mixed * (FULL / jnp.maximum(largest, 1e-30)))
+            part_out[k, c, p] = coded.astype(jnp.int32).astype(jnp.int16)
+            stat_out[k, c, p * 4 : p * 4 + 1, :] = peaks[p]
+            stat_out[k, c, p * 4 + 1 : p * 4 + 2, :] = totals[p]
+            stat_out[k, c, p * 4 + 2 : p * 4 + 3, :] = largest * (1.0 / FULL)
+            stat_out[k, c, p * 4 + 3 : p * 4 + 4, :] = jnp.zeros((1, 256), jnp.float32)
+
+        @pl.when(k > 0)
+        def _():
+            stat_copy(k, c, target).start()
+            part_copy(k, c, target).start()
+
+        return carry
+
+    lax.fori_loop(0, 2 * count, serve, 0)
+
+    for c in range(2):
+        for k in range(1, count):
+            stat_copy(k, c, partners[k]).wait_recv()
+            part_copy(k, c, partners[k]).wait_recv()
+        for p in range(2):
+            stats = [stat_out[0, c]] + [stat_in[k, c] for k in range(1, count)]
+            parts = [part_out[0, c, p]] + [part_in[k, c, p] for k in range(1, count)]
+            local_peak = local_stat[c, p, 0:1, :]
+            peak = local_peak
+            for stat in stats:
+                peak = jnp.maximum(peak, stat[p * 4 : p * 4 + 1])
+            share = jnp.exp(local_peak - peak)
+            total = share * local_stat[c, p, 1:2, :]
+            mixed = local_sum[c, p] * share
+            for stat, part in zip(stats, parts):
+                share = jnp.exp(stat[p * 4 : p * 4 + 1] - peak)
+                total = total + share * stat[p * 4 + 1 : p * 4 + 2]
+                weight = share * stat[p * 4 + 2 : p * 4 + 3]
+                mixed = mixed + part.astype(jnp.int32).astype(jnp.float32) * weight
+            turned[p, c] = (mixed / total).T.reshape(2, 16, 8, 128)
+    for p in range(2):
+        both = jnp.concatenate([turned[p, 0], turned[p, 1]], axis=2)
+        out_ref[:, p * 16 : p * 16 + 16] = both.astype(jnp.bfloat16)
+
+    for k in range(1, count):
+        ask_copy(k, partners[k]).wait_send()
+        for c in range(2):
+            query_copy(k, c, partners[k]).wait_send()
+            stat_copy(k, c, partners[k]).wait_send()
+            part_copy(k, c, partners[k]).wait_send()
+
+
+def move_queries(
+    page_pool, page_scales, queries, new_entries, token_cache, cache_fill, page_counts, page_table
+):
+    count = lax.axis_size("pre")
+    pool_rows = page_pool.shape[0]
+    capacity = pool_rows // count
+    width = queries.shape[-1]
+    requests = pl.pallas_call(
+        functools.partial(request_kernel, pool_rows),
+        out_shape=jax.ShapeDtypeStruct((count, 128), jnp.int32),
+        in_specs=[pl.BlockSpec(memory_space=pltpu.SMEM)] * 2,
+        out_specs=pl.BlockSpec(memory_space=pltpu.SMEM),
+        scratch_shapes=[pltpu.SMEM((count,), jnp.int32)],
+    )(page_counts, page_table)
+    scales = page_scales.transpose(1, 2, 0).reshape(-1).astype(jnp.float32)
+    vmem = pl.BlockSpec(memory_space=pltpu.VMEM)
+    smem = pl.BlockSpec(memory_space=pltpu.SMEM)
+    dma = pltpu.SemaphoreType.DMA
+    f32, bf16 = jnp.float32, jnp.bfloat16
+    return pl.pallas_call(
+        functools.partial(attend_kernel, (count, capacity, 1.0 / math.sqrt(width))),
+        out_shape=jax.ShapeDtypeStruct(queries.shape, queries.dtype),
+        in_specs=[vmem, smem, smem, vmem, vmem, vmem, pl.BlockSpec(memory_space=pl.ANY)],
+        out_specs=vmem,
+        scratch_shapes=[
+            pltpu.VMEM((pool_rows, 512, 128), bf16),
+            pltpu.VMEM((pool_rows, 2, 128, 128), bf16),
+            pltpu.VMEM((pool_rows, 2, 128, 128), bf16),
+            pltpu.VMEM((count, 1, 128), jnp.int32),
+            pltpu.SMEM((count, 1, 128), jnp.int32),
+            pltpu.VMEM((count, 2, 2, 256, 128), bf16),
+            pltpu.VMEM((2, 256, 128), bf16),
+            pltpu.VMEM((capacity, 128, 256), f32),
+            pltpu.VMEM((2, 128, 256), f32),
+            pltpu.VMEM((count, 2, 2, 128, 256), jnp.int16),
+            pltpu.VMEM((count, 2, 2, 128, 256), jnp.int16),
+            pltpu.VMEM((count, 2, 8, 256), f32),
+            pltpu.VMEM((count, 2, 8, 256), f32),
+            pltpu.VMEM((2, 2, 128, 256), f32),
+            pltpu.VMEM((2, 2, 8, 256), f32),
+            pltpu.VMEM((2, 2, 2, 16, 8, 128), f32),
+            dma,
+            dma((count,)),
+            dma((count,)),
+            dma((count,)),
+            dma((count, 2)),
+            dma((count, 2)),
+            dma((count, 2)),
+            dma((count, 2)),
+            dma((count, 2)),
+            dma((count, 2)),
+        ],
+        compiler_params=pltpu.CompilerParams(
+            collective_id=0, has_side_effects=True, vmem_limit_bytes=40 * 1024 * 1024
+        ),
+    )(
+        requests.reshape(count, 1, 128),
+        scales,
+        cache_fill,
+        queries,
+        token_cache.reshape(-1, width),
+        new_entries.reshape(-1, width),
+        page_pool.reshape(pool_rows, -1, width),
+    )
+
+
+def shards(
+    page_pool, page_scales, queries, new_entries, token_cache, cache_fill, page_counts, page_table
+):
+    args = (
+        page_pool, page_scales, queries, new_entries, token_cache, cache_fill, page_counts, page_table,
+    )
+    count = lax.axis_size("pre")
+    capacity = page_pool.shape[0] // count
+    if count in (2, 4, 8) and capacity * page_pool[0].size > 2 * queries.size:
+        return move_queries(*args)
+    return move_pages(*args)
+
+
 def solution(mesh):
     in_specs = (
         P(("groups", "pre"), None, "dec", None, None),

time: 183 us -> 61.9 us (0.34)
  waiting for transfers between devices: 93.7 us -> 0 us
  Pallas kernels: 0 us -> 53.9 us
  other arithmetic: 24.4 us -> 0.68 us
  local copies, waits for them, and re-layouts: 29.2 us -> 7 us
  matrix products: 20.1 us -> 0 us
  starting transfers between devices: 14.5 us -> 0 us
    all_to_all x3 -> x0, waiting for transfers between devices: 93.7 us -> none  [the longest x1 88.2 us: shards(): lax.all_to_all(page_block, 'pre', split_axis=0, concat_axis=0, tiled=True)]
    pallas_call x0 -> x2, Pallas kernels: none -> 53.9 us  [the longest x1 52.1 us: move_queries(): pl.pallas_call(functools.partial(attend_kernel, (count, capacity, 1.0 / m...]
    gather x9 -> x0, local copies, waits for them, and re-layouts: 24.8 us -> none  [the longest x1 12.3 us: pick_pages(): jnp.take(page_pool, flat_rows, axis=0)]
    dot_general x10 -> x0, matrix products: 20.1 us -> none  [the longest x2 8.66 us: prompt_block(): jnp.einsum('ctsgd,jicd->ctsgji', prompt_query, chosen[:, :, :, 0, :], pre...]
    all_to_all x3 -> x0, starting transfers between devices: 14.5 us -> none  [the longest x1 6.32 us: shards(): lax.all_to_all(requests, 'pre', split_axis=0, concat_axis=0, tiled=True)]
    reduce_sum x8 -> x0, other arithmetic: 12.3 us -> none  [the longest x2 11.4 us: prompt_block(): denominator = denominator[0] + jnp.sum(prefix_exp, axis=(-2, -1))]
    select_n x8 -> x0, other arithmetic: 9.92 us -> none  [the longest x4 5.11 us: prompt_block(): chosen = jnp.take(arrived, page_spot, axis=0)]
    unnamed x15 -> x13, local copies, waits for them, and re-layouts: 0.85 us -> 6.92 us
  transfers between devices with their start and end apart: 3 -> 0, of which waited for: 3 -> 0; matrix products, arithmetic and copies ran while one was open for 5% -> 0% of each run, Pallas kernels for 0% -> 0%
where the time goes in v1:
time: 61.9 us; the launch traced here: 61.6 us
  Pallas kernels  53.9 us (87%)
  local copies, waits for them, and re-layouts  7 us (11%)
  other arithmetic  0.68 us (1%)
    pallas_call x1, Pallas kernels, move_queries(): pl.pallas_call(functools.partial(attend_kernel, (count, capacity, 1.0 / m...  52.1 us
    unnamed x13, local copies, waits for them, and re-layouts  6.92 us
    pallas_call x1, Pallas kernels, move_queries(): pl.pallas_call(functools.partial(request_kernel, pool_rows), out_shape=ja...  1.81 us

profile of v1, /device:TPU:0, one launch (start us, length us, event | category | flops | bytes accessed | tf_op | source)
XLA Modules:
  0.0 61.6 jit_solution(15016336289874650179)
XLA Ops:
  0.0 0.7 %convert_bitcast_fusion = f32[2,2,32]{2,1,0:T(2,128)S(1)} fusion(bf16[32,2,2]{0,2,1:T(2,128)(2,1)} %param.9), kind=kLoop, calls=%fused_computation | loop fusion | flops 128 | bytes 768 | tf_op jit(solution)/shard_map/convert_element_type | solution.py:486
  0.7 0.1 reshape.19.scale_ref
  0.8 1.8 %shard_map.82 = s32[4,128]{1,0:T(4,128)} custom-call(s32[1,2]{1,0:T(1,128)} %counts_ref.1, s32[1,2,30]{2,1,0:T(2,128)} %table_ref.1), custom_call_target="tpu_custom_call" | custom-call | tf_op jit(solution)/shard_map/pallas_call | solution.py:479
  2.6 0.0 copy-start
  2.6 2.2 %copy-done = bf16[32,128,2,2,128]{4,3,2,1,0:T(2,128)(2,1)S(1)} copy-done((bf16[32,128,2,2,128]{4,3,2,1,0:T(2,128)(2,1)S(1)}, bf16[32,128,2,2,128]{4,3,2,1,0:T(2,128)(2,1)}, u32[]{:S(2)}) %copy-start) | copy-done | bytes 4194328
  4.8 0.0 copy-start.1
  4.8 0.9 %copy-done.1 = bf16[2,32,16,128]{3,2,1,0:T(8,128)(2,1)S(1)} copy-done((bf16[2,32,16,128]{3,2,1,0:T(8,128)(2,1)S(1)}, bf16[2,32,16,128]{3,2,1,0:T(8,128)(2,1)}, u32[]{:S(2)}) %copy-start.1) | copy-done | bytes 262168
  5.7 0.0 copy-start.2
  5.7 0.9 %copy-done.2 = bf16[32,4,2,2,128]{4,3,2,1,0:T(2,128)(2,1)S(1)} copy-done((bf16[32,4,2,2,128]{4,3,2,1,0:T(2,128)(2,1)S(1)}, bf16[32,4,2,2,128]{4,3,2,1,0:T(2,128)(2,1)}, u32[]{:S(2)}) %copy-start.2) | copy-done | bytes 131096
  6.6 0.0 copy-start.3
  6.6 0.8 %copy-done.3 = bf16[2,32,2,2,128]{4,3,2,1,0:T(2,128)(2,1)S(1)} copy-done((bf16[2,32,2,2,128]{4,3,2,1,0:T(2,128)(2,1)S(1)}, bf16[2,32,2,2,128]{4,3,2,1,0:T(2,128)(2,1)}, u32[]{:S(2)}) %copy-start.3) | copy-done | bytes 65560
  7.5 0.0 copy-start.4
  7.5 0.7 %copy-done.4 = s32[4,128]{1,0:T(4,128)S(1)} copy-done((s32[4,128]{1,0:T(4,128)S(1)}, s32[4,128]{1,0:T(4,128)}, u32[]{:S(2)}) %copy-start.4) | copy-done | bytes 2072
  8.2 0.0 copy-start.5
  8.2 0.7 %copy-done.5 = s32[32]{0:T(128)S(1)} copy-done((s32[32]{0:T(128)S(1)}, s32[32]{0:T(128)}, u32[]{:S(2)}) %copy-start.5) | copy-done | bytes 152
  8.8 52.1 %shard_map.83 = bf16[2,32,16,128]{3,2,1,0:T(8,128)(2,1)S(1)} custom-call(s32[4,1,128]{2,1,0:T(1,128)S(1)} %bitcast.9, f32[128]{0:T(128)S(1)} %reshape.19.scale_ref, s32[32]{0:T(128)S(1)} %copy-done.5, bf16[2,32,16,128]{3,2,1,0:T(8,128)(2,1)S(1)} %copy-done.1, bf16[512,128]{1,0:T(8,128)(2,1)S(1)} %bitcast.7, bf16[256,128]{1,0:T(8,128)(2,1)S(1)} %bitcast.8, ...), custom_call_target="tpu_custom_call" | custom-call | tf_op jit(solution)/shard_map/pallas_call | solution.py:491
  60.9 0.7 %copy.10 = bf16[2,32,16,128]{3,2,1,0:T(8,128)(2,1)} copy(bf16[2,32,16,128]{3,2,1,0:T(8,128)(2,1)S(1)} %shard_map.83) | data formatting | bytes 524288
Async XLA Ops:
  2.6 2.2 %copy-start = (bf16[32,128,2,2,128]{4,3,2,1,0:T(2,128)(2,1)S(1)}, bf16[32,128,2,2,128]{4,3,2,1,0:T(2,128)(2,1)}, u32[]{:S(2)}) copy-start(bf16[32,128,2,2,128]{4,3,2,1,0:T(2,128)(2,1)} %param.8) | copy-start | bytes 12582916
  4.8 0.9 %copy-start.1 = (bf16[2,32,16,128]{3,2,1,0:T(8,128)(2,1)S(1)}, bf16[2,32,16,128]{3,2,1,0:T(8,128)(2,1)}, u32[]{:S(2)}) copy-start(bf16[2,32,16,128]{3,2,1,0:T(8,128)(2,1)} %queries_ref.1) | copy-start | bytes 786436
  5.7 0.9 %copy-start.2 = (bf16[32,4,2,2,128]{4,3,2,1,0:T(2,128)(2,1)S(1)}, bf16[32,4,2,2,128]{4,3,2,1,0:T(2,128)(2,1)}, u32[]{:S(2)}) copy-start(bf16[32,4,2,2,128]{4,3,2,1,0:T(2,128)(2,1)} %param.12) | copy-start | bytes 393220
  6.6 0.8 %copy-start.3 = (bf16[2,32,2,2,128]{4,3,2,1,0:T(2,128)(2,1)S(1)}, bf16[2,32,2,2,128]{4,3,2,1,0:T(2,128)(2,1)}, u32[]{:S(2)}) copy-start(bf16[2,32,2,2,128]{4,3,2,1,0:T(2,128)(2,1)} %param.11) | copy-start | bytes 196612
  7.5 0.7 %copy-start.4 = (s32[4,128]{1,0:T(4,128)S(1)}, s32[4,128]{1,0:T(4,128)}, u32[]{:S(2)}) copy-start(s32[4,128]{1,0:T(4,128)} %shard_map.82) | copy-start | bytes 6148
  8.2 0.7 %copy-start.5 = (s32[32]{0:T(128)S(1)}, s32[32]{0:T(128)}, u32[]{:S(2)}) copy-start(s32[32]{0:T(128)} %fill_ref.1) | copy-start | bytes 388

commit v2 on v1

--- a/solution.py
+++ b/solution.py
@@ -179,20 +179,25 @@
     return result
 
 
-def request_kernel(pool_rows, counts_ref, table_ref, out_ref, rank_ref):
-    for owner in range(out_ref.shape[0]):
-        rank_ref[owner] = 0
-    for prompt in range(table_ref.shape[1]):
-
-        def place(j, carry, prompt=prompt):
-            page = table_ref[0, prompt, j]
-            owner = page // pool_rows
-            rank = rank_ref[owner]
-            out_ref[owner, rank] = (page - owner * pool_rows) * 2 + prompt
-            rank_ref[owner] = rank + 1
-            return carry
-
-        lax.fori_loop(0, counts_ref[0, prompt], place, 0)
+def wanted_slots(counts, table, pool_rows):
+    prompts, page_most = table.shape[1:]
+    rows = lax.broadcasted_iota(jnp.int32, (8, 128), 0)
+    lanes = lax.broadcasted_iota(jnp.int32, (8, 128), 1)
+    carry = (jnp.zeros((8, 128), jnp.int32), jnp.zeros((8, 128), jnp.int32))
+    for prompt in range(prompts):
+        length = counts[0, prompt]
+
+        def place(j, carry, prompt=prompt, length=length):
+            listed, ranks = carry
+            page = table[0, prompt, j]
+            owner = jnp.where(j < length, page // pool_rows, -1)
+            hit = rows == owner
+            code = (page - owner * pool_rows) * 2 + prompt
+            listed = jnp.where(hit & (ranks == lanes), code, listed)
+            return listed, jnp.where(hit, ranks + 1, ranks)
+
+        carry = lax.fori_loop(0, page_most, place, carry)
+    return carry[0]
 
 
 def nt_dot(a, b):
@@ -201,14 +206,25 @@
 
 def attend_kernel(
     dims,
-    request_ref,
+    counts_hbm,
+    table_hbm,
+    scale_hbm,
+    fill_hbm,
+    queries_hbm,
+    cache_hbm,
+    fresh_hbm,
+    pool_hbm,
+    out_ref,
+    counts_ref,
+    table_ref,
+    scale_raw,
+    scale_wide,
     scale_ref,
     fill_ref,
     queries_ref,
     cache_ref,
     fresh_ref,
-    pool_ref,
-    out_ref,
+    request_ref,
     raw,
     keys,
     values,
@@ -225,7 +241,7 @@
     local_sum,
     local_stat,
     turned,
-    pool_sem,
+    load_sem,
     smem_sem,
     ask_send,
     ask_recv,
@@ -244,11 +260,21 @@
     barrier = pltpu.get_barrier_semaphore()
     for k in range(1, count):
         pl.semaphore_signal(barrier, inc=1, device_id={"pre": partners[k]}, device_id_type=MESH)
-    pool_copy = pltpu.make_async_copy(pool_ref, raw, pool_sem)
-    pool_copy.start()
-    own_ask = pltpu.make_async_copy(request_ref.at[me], asked_smem.at[0], smem_sem.at[0])
-    own_ask.start()
-
+    pairs = (
+        (queries_hbm, queries_ref),
+        (table_hbm, table_ref),
+        (counts_hbm, counts_ref),
+        (fresh_hbm, fresh_ref),
+        (cache_hbm, cache_ref),
+        (fill_hbm, fill_ref),
+        (scale_hbm, scale_raw),
+        (pool_hbm, raw),
+    )
+    loads = [pltpu.make_async_copy(a, b, load_sem.at[i]) for i, (a, b) in enumerate(pairs)]
+    for load in loads:
+        load.start()
+    load_queries, load_table, load_counts, load_fresh, load_cache, load_fill, load_scale, load_pool = loads
+    load_queries.wait()
     for prompt in range(2):
         for step in range(2):
             block = queries_ref[step, prompt * 16 : prompt * 16 + 16].astype(jnp.float32)
@@ -299,11 +325,25 @@
             device_id_type=MESH,
         )
 
-    for k in range(1, count):
-        ask_copy(k, partners[k]).start()
     for c in range(2):
         for k in range(1, count):
             query_copy(k, c, partners[k]).start()
+    load_table.wait()
+    load_counts.wait()
+    listed = wanted_slots(counts_ref, table_ref, pages)
+    for owner in range(count):
+        request_ref[owner] = listed[owner : owner + 1]
+    for k in range(1, count):
+        ask_copy(k, partners[k]).start()
+    own_ask = pltpu.make_async_copy(request_ref.at[me], asked_smem.at[0], smem_sem.at[0])
+    own_ask.start()
+    load_scale.wait()
+    scale_wide[...] = scale_raw[...].astype(jnp.float32)
+    widen = pltpu.make_async_copy(scale_wide, scale_ref, load_sem.at[6])
+    widen.start()
+    load_fresh.wait()
+    load_cache.wait()
+    load_fill.wait()
 
     to_row = lax.broadcasted_iota(jnp.int32, (256, 256), 0)
     from_row = lax.broadcasted_iota(jnp.int32, (256, 256), 1)
@@ -359,7 +399,7 @@
                 preferred_element_type=jnp.float32,
             )
 
-    pool_copy.wait()
+    load_pool.wait()
 
     def sort_page(page, carry):
         halves = [sort_rows(raw[page, h * 256 : h * 256 + 256, :]) for h in range(2)]
@@ -375,6 +415,7 @@
 
     lax.fori_loop(0, pages, sort_page, 0)
     own_ask.wait()
+    widen.wait()
 
     def serve(index, carry):
         c, k = index // count, index % count
@@ -397,7 +438,7 @@
         prompts = [code % 2 for code in codes]
         peaks = [jnp.full((1, 256), LOW, jnp.float32) for _ in range(2)]
         for j in range(capacity):
-            key_scale = scale_ref[c * 2 * pages + slots[j]] * factor
+            key_scale = scale_ref[c, 0, slots[j]] * factor
             part = nt_dot(keys[slots[j], c], query_now[prompts[j]]) * key_scale
             scores[j] = part
             peak = jnp.max(part, axis=0, keepdims=True)
@@ -414,7 +455,7 @@
                 grown.astype(jnp.bfloat16),
                 preferred_element_type=jnp.float32,
             )
-            value_scale = scale_ref[(c * 2 + 1) * pages + slots[j]]
+            value_scale = scale_ref[c, 1, slots[j]]
             for p in range(2):
                 totals[p] = totals[p] + jnp.where(prompts[j] == p, total, 0.0)
                 sums[p] = sums[p] + mixed * jnp.where(prompts[j] == p, value_scale, 0.0)
@@ -476,24 +517,26 @@
     pool_rows = page_pool.shape[0]
     capacity = pool_rows // count
     width = queries.shape[-1]
-    requests = pl.pallas_call(
-        functools.partial(request_kernel, pool_rows),
-        out_shape=jax.ShapeDtypeStruct((count, 128), jnp.int32),
-        in_specs=[pl.BlockSpec(memory_space=pltpu.SMEM)] * 2,
-        out_specs=pl.BlockSpec(memory_space=pltpu.SMEM),
-        scratch_shapes=[pltpu.SMEM((count,), jnp.int32)],
-    )(page_counts, page_table)
-    scales = page_scales.transpose(1, 2, 0).reshape(-1).astype(jnp.float32)
     vmem = pl.BlockSpec(memory_space=pltpu.VMEM)
-    smem = pl.BlockSpec(memory_space=pltpu.SMEM)
+    hbm = pl.BlockSpec(memory_space=pltpu.HBM)
     dma = pltpu.SemaphoreType.DMA
     f32, bf16 = jnp.float32, jnp.bfloat16
     return pl.pallas_call(
         functools.partial(attend_kernel, (count, capacity, 1.0 / math.sqrt(width))),
         out_shape=jax.ShapeDtypeStruct(queries.shape, queries.dtype),
-        in_specs=[vmem, smem, smem, vmem, vmem, vmem, pl.BlockSpec(memory_space=pl.ANY)],
+        in_specs=[hbm] * 8,
         out_specs=vmem,
         scratch_shapes=[
+            pltpu.SMEM(page_counts.shape, jnp.int32),
+            pltpu.SMEM(page_table.shape, jnp.int32),
+            pltpu.VMEM((2, 2, pool_rows), bf16),
+            pltpu.VMEM((2, 2, pool_rows), f32),
+            pltpu.SMEM((2, 2, pool_rows), f32),
+            pltpu.SMEM(cache_fill.shape, jnp.int32),
+            pltpu.VMEM(queries.shape, bf16),
+            pltpu.VMEM((512, 128), bf16),
+            pltpu.VMEM((256, 128), bf16),
+            pltpu.VMEM((count, 1, 128), jnp.int32),
             pltpu.VMEM((pool_rows, 512, 128), bf16),
             pltpu.VMEM((pool_rows, 2, 128, 128), bf16),
             pltpu.VMEM((pool_rows, 2, 128, 128), bf16),
@@ -510,7 +553,7 @@
             pltpu.VMEM((2, 2, 128, 256), f32),
             pltpu.VMEM((2, 2, 8, 256), f32),
             pltpu.VMEM((2, 2, 2, 16, 8, 128), f32),
-            dma,
+            dma((8,)),
             dma((count,)),
             dma((count,)),
             dma((count,)),
@@ -522,11 +565,12 @@
             dma((count, 2)),
         ],
         compiler_params=pltpu.CompilerParams(
-            collective_id=0, has_side_effects=True, vmem_limit_bytes=40 * 1024 * 1024
+            collective_id=0, has_side_effects=True, vmem_limit_bytes=62 * 1024 * 1024
         ),
     )(
-        requests.reshape(count, 1, 128),
-        scales,
+        page_counts,
+        page_table,
+        page_scales.transpose(1, 2, 0),
         cache_fill,
         queries,
         token_cache.reshape(-1, width),

time: 61.9 us -> 53.5 us (0.86)
  local copies, waits for them, and re-layouts: 7 us -> 1.67 us
  Pallas kernels: 53.9 us -> 51.5 us
  other arithmetic: 0.68 us -> 0 us
    unnamed x13 -> x1, local copies, waits for them, and re-layouts: 6.92 us -> 1.67 us
    pallas_call x1 -> x0, Pallas kernels: 1.81 us -> none  [move_queries(): pl.pallas_call(functools.partial(request_kernel, pool_rows), out_shape=ja...]
    convert_element_type x1 -> x0, other arithmetic: 0.68 us -> none  [move_queries(): scales = page_scales.transpose(1, 2, 0).reshape(-1).astype(jnp.float32)]
where the time goes in v2:
time: 53.5 us; the launch traced here: 53.2 us
  Pallas kernels  51.5 us (96%)
  local copies, waits for them, and re-layouts  1.67 us (3%)
    pallas_call x1, Pallas kernels, move_queries(): pl.pallas_call(functools.partial(attend_kernel, (count, capacity, 1.0 / m...  51.5 us
    unnamed x1, local copies, waits for them, and re-layouts  1.67 us

profile of v2, /device:TPU:0, one launch (start us, length us, event | category | flops | bytes accessed | tf_op | source)
XLA Modules:
  0.0 53.2 jit_solution(4948978770297411193)
XLA Ops:
  0.0 51.5 %shard_map.82 = bf16[2,32,16,128]{3,2,1,0:T(8,128)(2,1)} custom-call(s32[1,2]{1,0:T(1,128)} %counts_hbm.1, s32[1,2,30]{2,1,0:T(2,128)} %table_hbm.1, bf16[2,2,32]{2,1,0:T(2,128)(2,1)} %bitcast.7, s32[32]{0:T(128)} %fill_hbm.1, bf16[2,32,16,128]{3,2,1,0:T(8,128)(2,1)} %queries_hbm.1, bf16[512,128]{1,0:T(8,128)(2,1)} %bitcast.5, bf16[256,128]{1,0:T(8,128)(2,1)} %bitcast.6, ...), custom_call_target="tpu_custom_call" | custom-call | tf_op jit(solution)/shard_map/pallas_call | solution.py:524
  51.5 1.7 %copy.10 = bf16[2,32,16,128]{3,2,1,0:T(8,128)(2,1)} copy(bf16[2,32,16,128]{3,2,1,0:T(8,128)(2,1)} %shard_map.82) | data formatting | bytes 524288

commit v3 on v2

--- a/solution.py
+++ b/solution.py
@@ -169,14 +169,6 @@
 MESH = pl.DeviceIdType.MESH
 LOW = -1e30
 FULL = 32000.0
-
-
-def partner_of(me, k, count):
-    bit, result = 1, 0
-    while bit < count:
-        result = result + ((me // bit) % 2 + (k // bit) % 2) % 2 * bit
-        bit *= 2
-    return result
 
 
 def wanted_slots(counts, table, pool_rows):
@@ -234,6 +226,7 @@
     query_now,
     scores,
     sums,
+    sum_stat,
     part_out,
     part_in,
     stat_out,
@@ -255,11 +248,11 @@
     count, capacity, factor = dims
     pages = raw.shape[0]
     me = lax.axis_index("pre")
-    partners = [partner_of(me, k, count) for k in range(count)]
+    others = [lax.rem(me + k, count) for k in range(1, count)]
 
     barrier = pltpu.get_barrier_semaphore()
-    for k in range(1, count):
-        pl.semaphore_signal(barrier, inc=1, device_id={"pre": partners[k]}, device_id_type=MESH)
+    for other in others:
+        pl.semaphore_signal(barrier, inc=1, device_id={"pre": other}, device_id_type=MESH)
     pairs = (
         (queries_hbm, queries_ref),
         (table_hbm, table_ref),
@@ -280,62 +273,82 @@
             block = queries_ref[step, prompt * 16 : prompt * 16 + 16].astype(jnp.float32)
             for c in range(2):
                 rows = block[:, c * 8 : c * 8 + 8, :].reshape(128, 128)
-                query_slots[0, c, prompt, step * 128 : step * 128 + 128, :] = rows.astype(
+                query_slots[me, c, prompt, step * 128 : step * 128 + 128, :] = rows.astype(
                     jnp.bfloat16
                 )
     pl.semaphore_wait(barrier, count - 1)
 
-    def ask_copy(k, target):
+    def ask_copy(source, target):
         return pltpu.make_async_remote_copy(
             src_ref=request_ref.at[target],
-            dst_ref=asked.at[k],
-            send_sem=ask_send.at[k],
-            recv_sem=ask_recv.at[k],
+            dst_ref=asked.at[source],
+            send_sem=ask_send.at[target],
+            recv_sem=ask_recv.at[source],
             device_id={"pre": target},
             device_id_type=MESH,
         )
 
-    def query_copy(k, c, target):
+    def query_copy(group, c, way):
         return pltpu.make_async_remote_copy(
-            src_ref=query_slots.at[0, c],
-            dst_ref=query_slots.at[k, c],
-            send_sem=query_send.at[k, c],
-            recv_sem=query_recv.at[k, c],
-            device_id={"pre": target},
+            src_ref=query_slots.at[group, c],
+            dst_ref=query_slots.at[group, c],
+            send_sem=query_send.at[group, c, way],
+            recv_sem=query_recv.at[group, c],
+            device_id={"pre": me + 1 - 2 * way},
             device_id_type=MESH,
         )
 
-    def part_copy(k, c, target):
+    def part_copy(group, c, way):
         return pltpu.make_async_remote_copy(
-            src_ref=part_out.at[k, c],
-            dst_ref=part_in.at[k, c],
-            send_sem=part_send.at[k, c],
-            recv_sem=part_recv.at[k, c],
-            device_id={"pre": target},
+            src_ref=part_out.at[group, c],
+            dst_ref=part_in.at[group + count * way, c],
+            send_sem=part_send.at[group, c],
+            recv_sem=part_recv.at[group + count * way, c],
+            device_id={"pre": me + 1 - 2 * way},
             device_id_type=MESH,
         )
 
-    def stat_copy(k, c, target):
+    def stat_copy(group, c, way):
         return pltpu.make_async_remote_copy(
-            src_ref=stat_out.at[k, c],
-            dst_ref=stat_in.at[k, c],
-            send_sem=stat_send.at[k, c],
-            recv_sem=stat_recv.at[k, c],
-            device_id={"pre": target},
+            src_ref=stat_out.at[group, c],
+            dst_ref=stat_in.at[group + count * way, c],
+            send_sem=stat_send.at[group, c],
+            recv_sem=stat_recv.at[group + count * way, c],
+            device_id={"pre": me + 1 - 2 * way},
             device_id_type=MESH,
         )
 
-    for c in range(2):
-        for k in range(1, count):
-            query_copy(k, c, partners[k]).start()
+    def has_next(way):
+        return me < count - 1 if way == 0 else me > 0
+
+    def send_queries(c):
+        for way in range(2):
+
+            @pl.when(has_next(way))
+            def _(way=way):
+                query_copy(me, c, way).start()
+
+    def take_queries(c, distance):
+        for way in range(2):
+            group = me - distance if way == 0 else me + distance
+
+            @pl.when((group >= 0) & (group < count))
+            def _(way=way, group=group):
+                query_copy(group, c, way).wait_recv()
+
+                @pl.when(has_next(way))
+                def _():
+                    query_copy(group, c, way).start()
+
+    send_queries(0)
     load_table.wait()
     load_counts.wait()
     listed = wanted_slots(counts_ref, table_ref, pages)
     for owner in range(count):
         request_ref[owner] = listed[owner : owner + 1]
-    for k in range(1, count):
-        ask_copy(k, partners[k]).start()
-    own_ask = pltpu.make_async_copy(request_ref.at[me], asked_smem.at[0], smem_sem.at[0])
+    for other in others:
+        ask_copy(me, other).start()
+    own_ask = pltpu.make_async_copy(request_ref.at[me], asked_smem.at[me], smem_sem.at[me])
     own_ask.start()
     load_scale.wait()
     scale_wide[...] = scale_raw[...].astype(jnp.float32)
@@ -387,7 +400,7 @@
                     axis=0,
                 )
 
-            part = nt_dot(pick(0).astype(jnp.bfloat16), query_slots[0, c, prompt]) * factor
+            part = nt_dot(pick(0).astype(jnp.bfloat16), query_slots[me, c, prompt]) * factor
             part = jnp.where(present, part, LOW)
             peak = jnp.max(part, axis=0, keepdims=True)
             grown = jnp.exp(part - peak)
@@ -401,39 +414,71 @@
 
     load_pool.wait()
 
-    def sort_page(page, carry):
-        halves = [sort_rows(raw[page, h * 256 : h * 256 + 256, :]) for h in range(2)]
-        for c in range(2):
-            at = c * 128
-            keys[page, c] = jnp.concatenate([x[at : at + 64] for x in halves], axis=0).astype(
-                jnp.bfloat16
-            )
-            values[page, c] = jnp.concatenate(
-                [x[at + 64 : at + 128] for x in halves], axis=0
-            ).T.astype(jnp.bfloat16)
+    def sort_pages(block, carry):
+        for i in range(4):
+            page = block * 4 + i
+            sides = jnp.concatenate([raw[page, :256, :], raw[page, 256:, :]], axis=1)
+            rows = sort_rows(sides)
+            for c in range(2):
+                at = c * 128
+                keys[page, c, :64] = rows[at : at + 64, :128].astype(jnp.bfloat16)
+                keys[page, c, 64:] = rows[at : at + 64, 128:].astype(jnp.bfloat16)
+                held = rows[at + 64 : at + 128]
+                values[page, c] = jnp.concatenate(
+                    [held[:, :128], held[:, 128:]], axis=0
+                ).T.astype(jnp.bfloat16)
         return carry
 
-    lax.fori_loop(0, pages, sort_page, 0)
+    blocks = pages // 4
+    for turn in range(count):
+        lax.fori_loop(blocks * turn // count, blocks * (turn + 1) // count, sort_pages, 0)
+        if turn < count - 1:
+            take_queries(0, turn + 1)
+        if turn == count // 2 - 1:
+            send_queries(1)
     own_ask.wait()
     widen.wait()
-
-    def serve(index, carry):
-        c, k = index // count, index % count
-        target = partner_of(me, k, count)
-
-        @pl.when((c == 0) & (k > 0))
-        def _():
-            ask_copy(k, target).wait_recv()
-            to_smem = pltpu.make_async_copy(asked.at[k], asked_smem.at[k], smem_sem.at[k])
-            to_smem.start()
-            to_smem.wait()
-
-        @pl.when(k > 0)
-        def _():
-            query_copy(k, c, target).wait_recv()
-
-        query_now[...] = query_slots[k, c]
-        codes = [asked_smem[k, 0, j] for j in range(capacity)]
+    for other in others:
+        ask_copy(other, me).wait_recv()
+        to_smem = pltpu.make_async_copy(asked.at[other], asked_smem.at[other], smem_sem.at[other])
+        to_smem.start()
+        to_smem.wait()
+
+    def code_and_send(group, c, way):
+        for p in range(2):
+            mixed = sums[group, c, p]
+            largest = jnp.max(jnp.abs(mixed), axis=0, keepdims=True)
+            coded = jnp.round(mixed * (FULL / jnp.maximum(largest, 1e-30)))
+            part_out[group, c, p] = coded.astype(jnp.int32).astype(jnp.int16)
+            stat_out[group, c, p * 4 : p * 4 + 2, :] = sum_stat[group, c, p * 4 : p * 4 + 2, :]
+            stat_out[group, c, p * 4 + 2 : p * 4 + 3, :] = largest * (1.0 / FULL)
+            stat_out[group, c, p * 4 + 3 : p * 4 + 4, :] = jnp.zeros((1, 256), jnp.float32)
+        stat_copy(group, c, way).start()
+        part_copy(group, c, way).start()
+
+    def add_incoming(group, c, way):
+        stat_copy(group, c, way).wait_recv()
+        part_copy(group, c, way).wait_recv()
+        slot = group + count * way
+        for p in range(2):
+            at = p * 4
+            there = stat_in[slot, c, at : at + 1, :]
+            here = sum_stat[group, c, at : at + 1, :]
+            peak = jnp.maximum(here, there)
+            keep, add = jnp.exp(here - peak), jnp.exp(there - peak)
+            sum_stat[group, c, at : at + 1, :] = peak
+            sum_stat[group, c, at + 1 : at + 2, :] = (
+                sum_stat[group, c, at + 1 : at + 2, :] * keep
+                + stat_in[slot, c, at + 1 : at + 2, :] * add
+            )
+            part = part_in[slot, c, p].astype(jnp.int32).astype(jnp.float32)
+            sums[group, c, p] = sums[group, c, p] * keep + part * (
+                add * stat_in[slot, c, at + 2 : at + 3, :]
+            )
+
+    def attend(group, c):
+        query_now[...] = query_slots[group, c]
+        codes = [asked_smem[group, 0, j] for j in range(capacity)]
         slots = [code // 2 for code in codes]
         prompts = [code % 2 for code in codes]
         peaks = [jnp.full((1, 256), LOW, jnp.float32) for _ in range(2)]
@@ -445,7 +490,7 @@
             for p in range(2):
                 peaks[p] = jnp.maximum(peaks[p], jnp.where(prompts[j] == p, peak, LOW))
         totals = [jnp.zeros((1, 256), jnp.float32) for _ in range(2)]
-        sums[...] = jnp.zeros_like(sums)
+        sums[group, c] = jnp.zeros((2, 128, 256), jnp.float32)
         for j in range(capacity):
             peak = jnp.where(prompts[j] == 0, peaks[0], peaks[1])
             grown = jnp.exp(scores[j] - peak)
@@ -458,56 +503,87 @@
             value_scale = scale_ref[c, 1, slots[j]]
             for p in range(2):
                 totals[p] = totals[p] + jnp.where(prompts[j] == p, total, 0.0)
-                sums[p] = sums[p] + mixed * jnp.where(prompts[j] == p, value_scale, 0.0)
+                sums[group, c, p] = sums[group, c, p] + mixed * jnp.where(prompts[j] == p, value_scale, 0.0)
         for p in range(2):
-            mixed = sums[p]
-            largest = jnp.max(jnp.abs(mixed), axis=0, keepdims=True)
-            coded = jnp.round(mixed * (FULL / jnp.maximum(largest, 1e-30)))
-            part_out[k, c, p] = coded.astype(jnp.int32).astype(jnp.int16)
-            stat_out[k, c, p * 4 : p * 4 + 1, :] = peaks[p]
-            stat_out[k, c, p * 4 + 1 : p * 4 + 2, :] = totals[p]
-            stat_out[k, c, p * 4 + 2 : p * 4 + 3, :] = largest * (1.0 / FULL)
-            stat_out[k, c, p * 4 + 3 : p * 4 + 4, :] = jnp.zeros((1, 256), jnp.float32)
-
-        @pl.when(k > 0)
+            sum_stat[group, c, p * 4 : p * 4 + 1, :] = peaks[p]
+            sum_stat[group, c, p * 4 + 1 : p * 4 + 2, :] = totals[p]
+
+    def serve(index, c):
+        way = index % 2
+        group = me + (1 - 2 * way) * (count - 1 - index // 2)
+
+        @pl.when((group >= 0) & (group < count) & (index < 2 * count - 1))
         def _():
-            stat_copy(k, c, target).start()
-            part_copy(k, c, target).start()
-
-        return carry
-
-    lax.fori_loop(0, 2 * count, serve, 0)
-
-    for c in range(2):
-        for k in range(1, count):
-            stat_copy(k, c, partners[k]).wait_recv()
-            part_copy(k, c, partners[k]).wait_recv()
+            attend(group, c)
+
+            @pl.when((group != me) & (me == way * (count - 1)))
+            def _():
+                code_and_send(group, c, way)
+
+        return c
+
+    def pass_on(c, passed):
+        for distance in range(count - 1 - passed, 0, -1):
+            for way in range(2):
+                group = me + (1 - 2 * way) * distance
+                behind = me if way == 0 else count - 1 - me
+
+                @pl.when((group >= 0) & (group < count) & (behind == passed))
+                def _(way=way, group=group):
+                    add_incoming(group, c, way)
+                    code_and_send(group, c, way)
+
+    def finish(c):
+        for way in range(2):
+
+            @pl.when(has_next(1 - way))
+            def _(way=way):
+                add_incoming(me, c, way)
+
         for p in range(2):
-            stats = [stat_out[0, c]] + [stat_in[k, c] for k in range(1, count)]
-            parts = [part_out[0, c, p]] + [part_in[k, c, p] for k in range(1, count)]
+            at = p * 4
+            here = sum_stat[me, c, at : at + 1, :]
             local_peak = local_stat[c, p, 0:1, :]
-            peak = local_peak
-            for stat in stats:
-                peak = jnp.maximum(peak, stat[p * 4 : p * 4 + 1])
-            share = jnp.exp(local_peak - peak)
-            total = share * local_stat[c, p, 1:2, :]
-            mixed = local_sum[c, p] * share
-            for stat, part in zip(stats, parts):
-                share = jnp.exp(stat[p * 4 : p * 4 + 1] - peak)
-                total = total + share * stat[p * 4 + 1 : p * 4 + 2]
-                weight = share * stat[p * 4 + 2 : p * 4 + 3]
-                mixed = mixed + part.astype(jnp.int32).astype(jnp.float32) * weight
-            turned[p, c] = (mixed / total).T.reshape(2, 16, 8, 128)
+            peak = jnp.maximum(here, local_peak)
+            keep, add = jnp.exp(here - peak), jnp.exp(local_peak - peak)
+            total = keep * sum_stat[me, c, at + 1 : at + 2, :] + add * local_stat[c, p, 1:2, :]
+            mixed = sums[me, c, p] * (keep / total) + local_sum[c, p] * (add / total)
+            turned[p, c] = mixed.T.reshape(2, 16, 8, 128)
+
+    lax.fori_loop(0, 2 * count - 1, serve, 0)
+    for distance in range(1, count):
+        take_queries(1, distance)
+        if distance == 1 and count > 2:
+            pass_on(0, 1)
+    lax.fori_loop(0, 2 * count - 1, serve, 1)
+    for passed in range(2, count - 1):
+        pass_on(0, passed)
+    finish(0)
+    for passed in range(1, count - 1):
+        pass_on(1, passed)
+    finish(1)
     for p in range(2):
         both = jnp.concatenate([turned[p, 0], turned[p, 1]], axis=2)
         out_ref[:, p * 16 : p * 16 + 16] = both.astype(jnp.bfloat16)
 
-    for k in range(1, count):
-        ask_copy(k, partners[k]).wait_send()
-        for c in range(2):
-            query_copy(k, c, partners[k]).wait_send()
-            stat_copy(k, c, partners[k]).wait_send()
-            part_copy(k, c, partners[k]).wait_send()
+    for other in others:
+        ask_copy(me, other).wait_send()
+    for c in range(2):
+        for way in range(2):
+            for distance in range(count):
+                group = me - distance if way == 0 else me + distance
+
+                @pl.when((group >= 0) & (group < count) & has_next(way))
+                def _(way=way, group=group, c=c):
+                    query_copy(group, c, way).wait_send()
+
+                target = me + distance if way == 0 else me - distance
+                if distance > 0:
+
+                    @pl.when((target >= 0) & (target < count))
+                    def _(way=way, target=target, c=c):
+                        stat_copy(target, c, way).wait_send()
+                        part_copy(target, c, way).wait_send()
 
 
 def move_queries(
@@ -545,11 +621,12 @@
             pltpu.VMEM((count, 2, 2, 256, 128), bf16),
             pltpu.VMEM((2, 256, 128), bf16),
             pltpu.VMEM((capacity, 128, 256), f32),
-            pltpu.VMEM((2, 128, 256), f32),
+            pltpu.VMEM((count, 2, 2, 128, 256), f32),
+            pltpu.VMEM((count, 2, 8, 256), f32),
             pltpu.VMEM((count, 2, 2, 128, 256), jnp.int16),
-            pltpu.VMEM((count, 2, 2, 128, 256), jnp.int16),
+            pltpu.VMEM((2 * count, 2, 2, 128, 256), jnp.int16),
             pltpu.VMEM((count, 2, 8, 256), f32),
-            pltpu.VMEM((count, 2, 8, 256), f32),
+            pltpu.VMEM((2 * count, 2, 8, 256), f32),
             pltpu.VMEM((2, 2, 128, 256), f32),
             pltpu.VMEM((2, 2, 8, 256), f32),
             pltpu.VMEM((2, 2, 2, 16, 8, 128), f32),
@@ -557,12 +634,12 @@
             dma((count,)),
             dma((count,)),
             dma((count,)),
+            dma((count, 2, 2)),
             dma((count, 2)),
             dma((count, 2)),
+            dma((2 * count, 2)),
             dma((count, 2)),
-            dma((count, 2)),
-            dma((count, 2)),
-            dma((count, 2)),
+            dma((2 * count, 2)),
         ],
         compiler_params=pltpu.CompilerParams(
             collective_id=0, has_side_effects=True, vmem_limit_bytes=62 * 1024 * 1024
@@ -587,7 +664,7 @@
     )
     count = lax.axis_size("pre")
     capacity = page_pool.shape[0] // count
-    if count in (2, 4, 8) and capacity * page_pool[0].size > 2 * queries.size:
+    if count in (2, 4, 8) and page_pool.shape[0] % (4 * count) == 0 and capacity * page_pool[0].size > 2 * queries.size:
         return move_queries(*args)
     return move_pages(*args)
 

time: 53.5 us -> 47.8 us (0.89)
  Pallas kernels: 51.5 us -> 45.9 us
    pallas_call x1, Pallas kernels: 51.5 us -> 45.9 us  [move_queries(): pl.pallas_call(functools.partial(attend_kernel, (count, capacity, 1.0 / m...]
where the time goes in v3:
time: 47.8 us; the launch traced here: 47.6 us
  Pallas kernels  45.9 us (96%)
  local copies, waits for them, and re-layouts  1.67 us (3%)
    pallas_call x1, Pallas kernels, move_queries(): pl.pallas_call(functools.partial(attend_kernel, (count, capacity, 1.0 / m...  45.9 us
    unnamed x1, local copies, waits for them, and re-layouts  1.67 us

profile of v3, /device:TPU:0, one launch (start us, length us, event | category | flops | bytes accessed | tf_op | source)
XLA Modules:
  0.0 47.6 jit_solution(1032252047559790055)
XLA Ops:
  0.0 45.9 %shard_map.82 = bf16[2,32,16,128]{3,2,1,0:T(8,128)(2,1)} custom-call(s32[1,2]{1,0:T(1,128)} %counts_hbm.1, s32[1,2,30]{2,1,0:T(2,128)} %table_hbm.1, bf16[2,2,32]{2,1,0:T(2,128)(2,1)} %bitcast.7, s32[32]{0:T(128)} %fill_hbm.1, bf16[2,32,16,128]{3,2,1,0:T(8,128)(2,1)} %queries_hbm.1, bf16[512,128]{1,0:T(8,128)(2,1)} %bitcast.5, bf16[256,128]{1,0:T(8,128)(2,1)} %bitcast.6, ...), custom_call_target="tpu_custom_call" | custom-call | tf_op jit(solution)/shard_map/pallas_call | solution.py:600
  45.9 1.7 %copy.10 = bf16[2,32,16,128]{3,2,1,0:T(8,128)(2,1)} copy(bf16[2,32,16,128]{3,2,1,0:T(8,128)(2,1)} %shard_map.82) | data formatting | bytes 524288

commit v4 on v3

--- a/solution.py
+++ b/solution.py
@@ -319,28 +319,25 @@
         )
 
     def has_next(way):
-        return me < count - 1 if way == 0 else me > 0
-
-    def send_queries(c):
-        for way in range(2):
-
-            @pl.when(has_next(way))
-            def _(way=way):
-                query_copy(me, c, way).start()
-
-    def take_queries(c, distance):
-        for way in range(2):
-            group = me - distance if way == 0 else me + distance
-
-            @pl.when((group >= 0) & (group < count))
-            def _(way=way, group=group):
-                query_copy(group, c, way).wait_recv()
-
-                @pl.when(has_next(way))
-                def _():
-                    query_copy(group, c, way).start()
-
-    send_queries(0)
+        ahead = me + 1 - 2 * way
+        return (ahead >= 0) & (ahead < count)
+
+    def send_queries(c, way, when):
+        @pl.when(when & has_next(way))
+        def _():
+            query_copy(me, c, way).start()
+
+    def take_queries(group, c, way):
+        query_copy(group, c, way).wait_recv()
+
+        @pl.when(has_next(way))
+        def _():
+            query_copy(group, c, way).start()
+
+    for way in range(2):
+        send_queries(0, way, me >= 0)
+    for way in range(2):
+        send_queries(1, way, me == way * (count - 1))
     load_table.wait()
     load_counts.wait()
     listed = wanted_slots(counts_ref, table_ref, pages)
@@ -365,6 +362,38 @@
     def sort_rows(block):
         return jnp.dot(order, block, preferred_element_type=jnp.float32)
 
+    load_pool.wait()
+
+    def sort_pages(block, carry):
+        for i in range(4):
+            page = block * 4 + i
+            sides = jnp.concatenate([raw[page, :256, :], raw[page, 256:, :]], axis=1)
+            rows = sort_rows(sides)
+            for c in range(2):
+                at = c * 128
+                keys[page, c, :64] = rows[at : at + 64, :128].astype(jnp.bfloat16)
+                keys[page, c, 64:] = rows[at : at + 64, 128:].astype(jnp.bfloat16)
+                held = rows[at + 64 : at + 128]
+                values[page, c] = jnp.concatenate(
+                    [held[:, :128], held[:, 128:]], axis=0
+                ).T.astype(jnp.bfloat16)
+        return carry
+
+    blocks = pages // 4
+    def take_near(distance):
+        for way in range(2):
+            group = me - (1 - 2 * way) * distance
+
+            @pl.when((group >= 0) & (group < count))
+            def _(way=way, group=group):
+                take_queries(group, 0, way)
+
+    lax.fori_loop(0, blocks // 2, sort_pages, 0)
+    take_near(1)
+    lax.fori_loop(blocks // 2, blocks, sort_pages, 0)
+    if count > 2:
+        take_near(2)
+
     fresh_block = jnp.concatenate(
         [
             fresh_ref[step * 128 + prompt * 64 : step * 128 + prompt * 64 + 64, :]
@@ -412,30 +441,6 @@
                 preferred_element_type=jnp.float32,
             )
 
-    load_pool.wait()
-
-    def sort_pages(block, carry):
-        for i in range(4):
-            page = block * 4 + i
-            sides = jnp.concatenate([raw[page, :256, :], raw[page, 256:, :]], axis=1)
-            rows = sort_rows(sides)
-            for c in range(2):
-                at = c * 128
-                keys[page, c, :64] = rows[at : at + 64, :128].astype(jnp.bfloat16)
-                keys[page, c, 64:] = rows[at : at + 64, 128:].astype(jnp.bfloat16)
-                held = rows[at + 64 : at + 128]
-                values[page, c] = jnp.concatenate(
-                    [held[:, :128], held[:, 128:]], axis=0
-                ).T.astype(jnp.bfloat16)
-        return carry
-
-    blocks = pages // 4
-    for turn in range(count):
-        lax.fori_loop(blocks * turn // count, blocks * (turn + 1) // count, sort_pages, 0)
-        if turn < count - 1:
-            take_queries(0, turn + 1)
-        if turn == count // 2 - 1:
-            send_queries(1)
     own_ask.wait()
     widen.wait()
     for other in others:
@@ -508,22 +513,40 @@
             sum_stat[group, c, p * 4 : p * 4 + 1, :] = peaks[p]
             sum_stat[group, c, p * 4 + 1 : p * 4 + 2, :] = totals[p]
 
-    def serve(index, c):
+    def serve(group, c, way):
+        attend(group, c)
+
+        @pl.when(jnp.logical_not(has_next(way)))
+        def _():
+            code_and_send(group, c, 1 - way)
+
+    def serve_near(taken, index, carry):
         way = index % 2
-        group = me + (1 - 2 * way) * (count - 1 - index // 2)
-
-        @pl.when((group >= 0) & (group < count) & (index < 2 * count - 1))
+        group = me - (1 - 2 * way) * (1 + index // 2)
+
+        @pl.when((group >= 0) & (group < count))
         def _():
-            attend(group, c)
-
-            @pl.when((group != me) & (me == way * (count - 1)))
-            def _():
-                code_and_send(group, c, way)
-
-        return c
+            if not taken:
+                take_queries(group, 0, way)
+            serve(group, 0, way)
+
+        return carry
+
+    def serve_far(behind, index, carry):
+        way, distance = index % 2, 1 + index // 2
+        group = me - (1 - 2 * way) * distance
+
+        @pl.when(group == behind * (1 - 2 * way) + (count - 1) * way)
+        def _():
+            take_queries(group, 1, way)
+            send_queries(1, way, distance == 1)
+            serve(group, 1, way)
+
+        return carry
 
     def pass_on(c, passed):
-        for distance in range(count - 1 - passed, 0, -1):
+        distances = range(1, count - passed)
+        for distance in distances if c == 0 else reversed(distances):
             for way in range(2):
                 group = me + (1 - 2 * way) * distance
                 behind = me if way == 0 else count - 1 - me
@@ -550,14 +573,18 @@
             mixed = sums[me, c, p] * (keep / total) + local_sum[c, p] * (add / total)
             turned[p, c] = mixed.T.reshape(2, 16, 8, 128)
 
-    lax.fori_loop(0, 2 * count - 1, serve, 0)
-    for distance in range(1, count):
-        take_queries(1, distance)
-        if distance == 1 and count > 2:
-            pass_on(0, 1)
-    lax.fori_loop(0, 2 * count - 1, serve, 1)
-    for passed in range(2, count - 1):
-        pass_on(0, passed)
+    def attend_own(c, carry):
+        attend(me, c)
+        return carry
+
+    lax.fori_loop(0, 2, attend_own, 0)
+    taken = 2 * min(2, count - 1)
+    lax.fori_loop(0, taken, functools.partial(serve_near, True), 0)
+    lax.fori_loop(taken, 2 * (count - 1), functools.partial(serve_near, False), 0)
+    for behind in range(count - 1):
+        lax.fori_loop(0, 2 * (count - 1 - behind), functools.partial(serve_far, behind), 0)
+        if behind + 1 < count - 1:
+            pass_on(0, behind + 1)
     finish(0)
     for passed in range(1, count - 1):
         pass_on(1, passed)

time: 47.8 us -> 46.2 us (0.967)
  Pallas kernels: 45.9 us -> 44.4 us
    pallas_call x1, Pallas kernels: 45.9 us -> 44.4 us  [move_queries(): pl.pallas_call(functools.partial(attend_kernel, (count, capacity, 1.0 / m...]
where the time goes in v4:
time: 46.2 us; the launch traced here: 46.1 us
  Pallas kernels  44.4 us (96%)
  local copies, waits for them, and re-layouts  1.67 us (4%)
    pallas_call x1, Pallas kernels, move_queries(): pl.pallas_call(functools.partial(attend_kernel, (count, capacity, 1.0 / m...  44.4 us
    unnamed x1, local copies, waits for them, and re-layouts  1.67 us

profile of v4, /device:TPU:0, one launch (start us, length us, event | category | flops | bytes accessed | tf_op | source)
XLA Modules:
  0.0 46.1 jit_solution(2484121507307316217)
XLA Ops:
  0.0 44.4 %shard_map.82 = bf16[2,32,16,128]{3,2,1,0:T(8,128)(2,1)} custom-call(s32[1,2]{1,0:T(1,128)} %counts_hbm.1, s32[1,2,30]{2,1,0:T(2,128)} %table_hbm.1, bf16[2,2,32]{2,1,0:T(2,128)(2,1)} %bitcast.7, s32[32]{0:T(128)} %fill_hbm.1, bf16[2,32,16,128]{3,2,1,0:T(8,128)(2,1)} %queries_hbm.1, bf16[512,128]{1,0:T(8,128)(2,1)} %bitcast.5, bf16[256,128]{1,0:T(8,128)(2,1)} %bitcast.6, ...), custom_call_target="tpu_custom_call" | custom-call | tf_op jit(solution)/shard_map/pallas_call | solution.py:627
  44.4 1.7 %copy.10 = bf16[2,32,16,128]{3,2,1,0:T(8,128)(2,1)} copy(bf16[2,32,16,128]{3,2,1,0:T(8,128)(2,1)} %shard_map.82) | data formatting | bytes 524288

commit v5 on v4

--- a/solution.py
+++ b/solution.py
@@ -322,8 +322,8 @@
         ahead = me + 1 - 2 * way
         return (ahead >= 0) & (ahead < count)
 
-    def send_queries(c, way, when):
-        @pl.when(when & has_next(way))
+    def send_queries(c, way):
+        @pl.when(has_next(way))
         def _():
             query_copy(me, c, way).start()
 
@@ -334,10 +334,9 @@
         def _():
             query_copy(group, c, way).start()
 
-    for way in range(2):
-        send_queries(0, way, me >= 0)
-    for way in range(2):
-        send_queries(1, way, me == way * (count - 1))
+    for c in range(2):
+        for way in range(2):
+            send_queries(c, way)
     load_table.wait()
     load_counts.wait()
     listed = wanted_slots(counts_ref, table_ref, pages)
@@ -380,19 +379,20 @@
         return carry
 
     blocks = pages // 4
-    def take_near(distance):
+    def take_all(distance, c):
         for way in range(2):
             group = me - (1 - 2 * way) * distance
 
             @pl.when((group >= 0) & (group < count))
             def _(way=way, group=group):
-                take_queries(group, 0, way)
+                take_queries(group, c, way)
 
     lax.fori_loop(0, blocks // 2, sort_pages, 0)
-    take_near(1)
+    take_all(1, 0)
     lax.fori_loop(blocks // 2, blocks, sort_pages, 0)
+    take_all(1, 1)
     if count > 2:
-        take_near(2)
+        take_all(2, 0)
 
     fresh_block = jnp.concatenate(
         [
@@ -520,41 +520,29 @@
         def _():
             code_and_send(group, c, 1 - way)
 
-    def serve_near(taken, index, carry):
-        way = index % 2
-        group = me - (1 - 2 * way) * (1 + index // 2)
+    def serve_next(index, carry):
+        distance, c, way = 1 + index // 4, index // 2 % 2, index % 2
+        group = me - (1 - 2 * way) * distance
 
         @pl.when((group >= 0) & (group < count))
         def _():
-            if not taken:
-                take_queries(group, 0, way)
-            serve(group, 0, way)
+            @pl.when(distance * 2 + c > 4)
+            def _():
+                take_queries(group, c, way)
+
+            serve(group, c, way)
 
         return carry
 
-    def serve_far(behind, index, carry):
-        way, distance = index % 2, 1 + index // 2
-        group = me - (1 - 2 * way) * distance
-
-        @pl.when(group == behind * (1 - 2 * way) + (count - 1) * way)
-        def _():
-            take_queries(group, 1, way)
-            send_queries(1, way, distance == 1)
-            serve(group, 1, way)
-
-        return carry
-
-    def pass_on(c, passed):
-        distances = range(1, count - passed)
-        for distance in distances if c == 0 else reversed(distances):
-            for way in range(2):
-                group = me + (1 - 2 * way) * distance
-                behind = me if way == 0 else count - 1 - me
-
-                @pl.when((group >= 0) & (group < count) & (behind == passed))
-                def _(way=way, group=group):
-                    add_incoming(group, c, way)
-                    code_and_send(group, c, way)
+    def pass_on(c, passed, distance):
+        for way in range(2):
+            group = me + (1 - 2 * way) * distance
+            behind = me if way == 0 else count - 1 - me
+
+            @pl.when((group >= 0) & (group < count) & (behind == passed))
+            def _(way=way, group=group):
+                add_incoming(group, c, way)
+                code_and_send(group, c, way)
 
     def finish(c):
         for way in range(2):
@@ -578,16 +566,12 @@
         return carry
 
     lax.fori_loop(0, 2, attend_own, 0)
-    taken = 2 * min(2, count - 1)
-    lax.fori_loop(0, taken, functools.partial(serve_near, True), 0)
-    lax.fori_loop(taken, 2 * (count - 1), functools.partial(serve_near, False), 0)
-    for behind in range(count - 1):
-        lax.fori_loop(0, 2 * (count - 1 - behind), functools.partial(serve_far, behind), 0)
-        if behind + 1 < count - 1:
-            pass_on(0, behind + 1)
+    lax.fori_loop(0, 4 * (count - 1), serve_next, 0)
+    for passed in range(1, count - 1):
+        for distance in range(1, count - passed):
+            for c in range(2):
+                pass_on(c, passed, distance)
     finish(0)
-    for passed in range(1, count - 1):
-        pass_on(1, passed)
     finish(1)
     for p in range(2):
         both = jnp.concatenate([turned[p, 0], turned[p, 1]], axis=2)

time: 46.2 us -> 49.6 us (1.074)
  Pallas kernels: 44.4 us -> 47.7 us
    pallas_call x1, Pallas kernels: 44.4 us -> 47.7 us  [move_queries(): pl.pallas_call(functools.partial(attend_kernel, (count, capacity, 1.0 / m...]
where the time goes in v5:
time: 49.6 us; the launch traced here: 49.4 us
  Pallas kernels  47.7 us (96%)
  local copies, waits for them, and re-layouts  1.67 us (3%)
    pallas_call x1, Pallas kernels, move_queries(): pl.pallas_call(functools.partial(attend_kernel, (count, capacity, 1.0 / m...  47.7 us
    unnamed x1, local copies, waits for them, and re-layouts  1.67 us

profile of v5, /device:TPU:0, one launch (start us, length us, event | category | flops | bytes accessed | tf_op | source)
XLA Modules:
  0.0 49.4 jit_solution(16740585097286387161)
XLA Ops:
  0.0 47.7 %shard_map.82 = bf16[2,32,16,128]{3,2,1,0:T(8,128)(2,1)} custom-call(s32[1,2]{1,0:T(1,128)} %counts_hbm.1, s32[1,2,30]{2,1,0:T(2,128)} %table_hbm.1, bf16[2,2,32]{2,1,0:T(2,128)(2,1)} %bitcast.7, s32[32]{0:T(128)} %fill_hbm.1, bf16[2,32,16,128]{3,2,1,0:T(8,128)(2,1)} %queries_hbm.1, bf16[512,128]{1,0:T(8,128)(2,1)} %bitcast.5, bf16[256,128]{1,0:T(8,128)(2,1)} %bitcast.6, ...), custom_call_target="tpu_custom_call" | custom-call | tf_op jit(solution)/shard_map/pallas_call | solution.py:611
  47.7 1.7 %copy.10 = bf16[2,32,16,128]{3,2,1,0:T(8,128)(2,1)} copy(bf16[2,32,16,128]{3,2,1,0:T(8,128)(2,1)} %shard_map.82) | data formatting | bytes 524288

commit v6 on v5

--- a/solution.py
+++ b/solution.py
@@ -288,13 +288,13 @@
             device_id_type=MESH,
         )
 
-    def query_copy(group, c, way):
+    def query_copy(group, c, target):
         return pltpu.make_async_remote_copy(
             src_ref=query_slots.at[group, c],
             dst_ref=query_slots.at[group, c],
-            send_sem=query_send.at[group, c, way],
+            send_sem=query_send.at[target, c],
             recv_sem=query_recv.at[group, c],
-            device_id={"pre": me + 1 - 2 * way},
+            device_id={"pre": target},
             device_id_type=MESH,
         )
 
@@ -322,21 +322,9 @@
         ahead = me + 1 - 2 * way
         return (ahead >= 0) & (ahead < count)
 
-    def send_queries(c, way):
-        @pl.when(has_next(way))
-        def _():
-            query_copy(me, c, way).start()
-
-    def take_queries(group, c, way):
-        query_copy(group, c, way).wait_recv()
-
-        @pl.when(has_next(way))
-        def _():
-            query_copy(group, c, way).start()
-
     for c in range(2):
-        for way in range(2):
-            send_queries(c, way)
+        for other in others:
+            query_copy(me, c, other).start()
     load_table.wait()
     load_counts.wait()
     listed = wanted_slots(counts_ref, table_ref, pages)
@@ -379,20 +367,7 @@
         return carry
 
     blocks = pages // 4
-    def take_all(distance, c):
-        for way in range(2):
-            group = me - (1 - 2 * way) * distance
-
-            @pl.when((group >= 0) & (group < count))
-            def _(way=way, group=group):
-                take_queries(group, c, way)
-
-    lax.fori_loop(0, blocks // 2, sort_pages, 0)
-    take_all(1, 0)
-    lax.fori_loop(blocks // 2, blocks, sort_pages, 0)
-    take_all(1, 1)
-    if count > 2:
-        take_all(2, 0)
+    lax.fori_loop(0, blocks, sort_pages, 0)
 
     fresh_block = jnp.concatenate(
         [
@@ -521,15 +496,13 @@
             code_and_send(group, c, 1 - way)
 
     def serve_next(index, carry):
-        distance, c, way = 1 + index // 4, index // 2 % 2, index % 2
+        distance, way = 1 + index // 2 % (count - 1), index % 2
+        c = index // (2 * (count - 1))
         group = me - (1 - 2 * way) * distance
 
         @pl.when((group >= 0) & (group < count))
         def _():
-            @pl.when(distance * 2 + c > 4)
-            def _():
-                take_queries(group, c, way)
-
+            query_copy(group, c, group).wait_recv()
             serve(group, c, way)
 
         return carry
@@ -579,15 +552,11 @@
 
     for other in others:
         ask_copy(me, other).wait_send()
+        for c in range(2):
+            query_copy(me, c, other).wait_send()
     for c in range(2):
         for way in range(2):
             for distance in range(count):
-                group = me - distance if way == 0 else me + distance
-
-                @pl.when((group >= 0) & (group < count) & has_next(way))
-                def _(way=way, group=group, c=c):
-                    query_copy(group, c, way).wait_send()
-
                 target = me + distance if way == 0 else me - distance
                 if distance > 0:
 
@@ -645,7 +614,7 @@
             dma((count,)),
             dma((count,)),
             dma((count,)),
-            dma((count, 2, 2)),
+            dma((count, 2)),
             dma((count, 2)),
             dma((count, 2)),
             dma((2 * count, 2)),

time: 49.6 us -> 64.8 us (1.31)
  Pallas kernels: 47.7 us -> 63 us
    pallas_call x1, Pallas kernels: 47.7 us -> 63 us  [move_queries(): pl.pallas_call(functools.partial(attend_kernel, (count, capacity, 1.0 / m...]
where the time goes in v6:
time: 64.8 us; the launch traced here: 64.7 us
  Pallas kernels  63 us (97%)
  local copies, waits for them, and re-layouts  1.67 us (3%)
    pallas_call x1, Pallas kernels, move_queries(): pl.pallas_call(functools.partial(attend_kernel, (count, capacity, 1.0 / m...  63 us
    unnamed x1, local copies, waits for them, and re-layouts  1.67 us

profile of v6, /device:TPU:0, one launch (start us, length us, event | category | flops | bytes accessed | tf_op | source)
XLA Modules:
  0.0 64.7 jit_solution(7050387547849762627)
XLA Ops:
  0.0 63.0 %shard_map.82 = bf16[2,32,16,128]{3,2,1,0:T(8,128)(2,1)} custom-call(s32[1,2]{1,0:T(1,128)} %counts_hbm.1, s32[1,2,30]{2,1,0:T(2,128)} %table_hbm.1, bf16[2,2,32]{2,1,0:T(2,128)(2,1)} %bitcast.7, s32[32]{0:T(128)} %fill_hbm.1, bf16[2,32,16,128]{3,2,1,0:T(8,128)(2,1)} %queries_hbm.1, bf16[512,128]{1,0:T(8,128)(2,1)} %bitcast.5, bf16[256,128]{1,0:T(8,128)(2,1)} %bitcast.6, ...), custom_call_target="tpu_custom_call" | custom-call | tf_op jit(solution)/shard_map/pallas_call | solution.py:580
  63.0 1.7 %copy.10 = bf16[2,32,16,128]{3,2,1,0:T(8,128)(2,1)} copy(bf16[2,32,16,128]{3,2,1,0:T(8,128)(2,1)} %shard_map.82) | data formatting | bytes 524288
